TPU v7x, 256 devices: a whole 4x4x8 slice. The times are simulated.
256 devices in a mesh: grp: 4 (over x), seq: 64 (over z, y, core).
Axes of the slice: x: 4, y: 4, z: 8, core: 2. Of those that a mesh axis runs over, the one named last changes fastest.
Arguments:
- queries: bfloat16 [4, 16384, 4096], P('grp', 'seq'), may hold values from -6 to 6
- key_base: bfloat16 [4, 16384, 512], P('grp', 'seq'), may hold values from -6 to 6
- value_base: bfloat16 [4, 16384, 512], P('grp', 'seq'), may hold values from -6 to 6
- out_grad: bfloat16 [4, 16384, 4096], P('grp', 'seq'), may hold values from -6 to 6
- doc_lengths: int32 [4, 128], P('grp'), may hold values from 1 to 512, 16384 in all within a row
- key_scale: float32 [512], replicated, may hold values from 0.5 to 1.5
- value_scale: float32 [512], replicated, may hold values from 0.5 to 1.5
Outputs:
- grad_queries: bfloat16 [4, 16384, 4096], P('grp', 'seq')
- grad_key_base: bfloat16 [4, 16384, 512], P('grp', 'seq')
- grad_value_base: bfloat16 [4, 16384, 512], P('grp', 'seq')
- grad_key_scale: float32 [512], replicated
- grad_value_scale: float32 [512], replicated
Inputs may be any that keep to these rules, and one draw needn't show every extreme that they name: `doc_lengths`: the lengths of one packed sequence sum to 16384; the largest is exactly 512.
All inputs are finite; a program needn't handle non-finite values.
Results may differ from a plain program's by a relative error of at most 0.012.
The roundings to bfloat16 on the way count: a program that leaves them out, or rounds other values in their place, can miss the bound.
Values may be sent and summed in bfloat16 or wider, within the bound.
No kernel may reach another device: no remote copies, remote signals or barrier semaphores. Data moves between devices by JAX's collectives and lax.ppermute only.
A program may use at most 128 MiB of HBM per device.

v0:
```python
import functools
import math

import jax
import jax.numpy as jnp
from jax import lax
from jax.experimental import pallas as pl
from jax.experimental.pallas import tpu as pltpu
from jax.sharding import PartitionSpec as P

HD = 128
REACH = 2
DOC_MOST = 512
QT = 128
KG = 128
LANES = 256
NEG = -1e30
F32 = jnp.float32
BF16 = jnp.bfloat16


def attend_kernel(
    info, dstart, kscale, vscale, q_ref, g_ref, k_own, v_own, far, near_a, near_b,
    dq_ref, own_ref, part_ref, sums_ref, bias, k_raw, v_raw, k_win, v_win, dk_acc, dv_acc,
):
    tok = k_own.shape[0]
    front = REACH * tok
    per_group = q_ref.shape[1] // HD
    packed = LANES // QT
    tiles = tok // QT
    most = (DOC_MOST + QT) // KG
    inv_root = 1.0 / math.sqrt(HD)
    log2_scale = inv_root * math.log2(math.e)

    @pl.when(pl.program_id(0) == 0)
    def _():
        k_pos = lax.broadcasted_iota(jnp.int32, (front + tok, LANES), 0)
        lane = lax.broadcasted_iota(jnp.int32, (front + tok, LANES), 1) % QT
        for tile in range(tiles):
            start = dstart[tile : tile + 1, :]
            q_pos = lane + (front + tile * QT)
            ok = (k_pos >= start) & (k_pos <= q_pos)
            bias[tile] = jnp.where(ok, 0.0, NEG)

    even = info[tiles] == 0
    k_raw[:tok] = far[:, :HD]
    v_raw[:tok] = far[:, HD:]
    near = jnp.where(even, near_b[...], near_a[...])
    k_raw[tok:front] = near[:, :HD]
    v_raw[tok:front] = near[:, HD:]
    k_raw[front:] = k_own[...]
    v_raw[front:] = v_own[...]
    k_win[...] = (k_raw[...].astype(F32) * kscale[...]).astype(BF16)
    v_win[...] = (v_raw[...].astype(F32) * vscale[...]).astype(BF16)
    dk_acc[...] = jnp.zeros_like(dk_acc)
    dv_acc[...] = jnp.zeros_like(dv_acc)

    nt = (((1,), (1,)), ((), ()))

    def one_tile(tile, units):
        row = pl.multiple_of(tile * QT, QT)
        count = units * KG
        low = pl.multiple_of(front + (tile + 1) * QT - count, KG)
        rows = pl.ds(low, count)
        keys = k_win[rows, :]
        values = v_win[rows, :]
        keys_t = keys.T
        mask = bias[tile, rows, :]
        dk = None
        dv = None
        for first in range(0, per_group, packed):
            cols = [slice((first + i) * HD, (first + i + 1) * HD) for i in range(packed)]
            q_part = jnp.concatenate([q_ref[pl.ds(row, QT), c] for c in cols], axis=0)
            g_part = jnp.concatenate([g_ref[pl.ds(row, QT), c] for c in cols], axis=0)
            scores = lax.dot_general(keys, q_part, nt, preferred_element_type=F32)
            dprobs = lax.dot_general(values, g_part, nt, preferred_element_type=F32)
            scores = scores * log2_scale + mask
            peak = jnp.max(scores, axis=0, keepdims=True)
            raised = jnp.exp2(scores - peak)
            inverse = 1.0 / jnp.sum(raised, axis=0, keepdims=True)
            weights = raised * inverse
            delta = jnp.sum(weights * dprobs, axis=0, keepdims=True)
            probs = weights.astype(BF16)
            dscores = (weights * (dprobs - delta)).astype(BF16)
            dv_one = jnp.dot(probs, g_part, preferred_element_type=F32)
            dk_one = jnp.dot(dscores, q_part, preferred_element_type=F32)
            dv = dv_one if dv is None else dv + dv_one
            dk = dk_one if dk is None else dk + dk_one
            dq_t = jnp.dot(keys_t, dscores, preferred_element_type=F32) * inv_root
            dq = dq_t.T.astype(BF16)
            for i, c in enumerate(cols):
                dq_ref[pl.ds(row, QT), c] = dq[i * QT : (i + 1) * QT]
        dk_acc[rows, :] += dk
        dv_acc[rows, :] += dv

    def tile_step(tile, carry):
        units = info[tile]
        for static in range(1, most + 1):
            pl.when(units == static)(functools.partial(one_tile, tile, static))
        return carry

    lax.fori_loop(0, tiles, tile_step, 0)
    dk = dk_acc[...] * inv_root
    dv = dv_acc[...]
    own_ref[:, :HD] = dk[front:]
    own_ref[:, HD:] = dv[front:]
    part_ref[:, :HD] = dk[:front].astype(BF16)
    part_ref[:, HD:] = dv[:front].astype(BF16)
    sums_ref[0, 0:1, :] = jnp.sum(dk * k_raw[...].astype(F32), axis=0, keepdims=True)
    sums_ref[0, 1:2, :] = jnp.sum(dv * v_raw[...].astype(F32), axis=0, keepdims=True)


def attend(heads, first, info, dstart, kscale, vscale, q, g, k_own, v_own, far, near_a, near_b):
    tok = k_own.shape[0]
    span = (REACH + 1) * tok
    group = q.shape[1] * HD // k_own.shape[1]
    tiles = tok // QT

    def at(width, offset):
        return pl.BlockSpec((tok, width), lambda h: (0, h + offset))

    vec = pl.BlockSpec((1, HD), lambda h: (0, h + first))
    out_shape = (
        jax.ShapeDtypeStruct((tok, heads * group), BF16),
        jax.ShapeDtypeStruct((tok, heads * 2 * HD), F32),
        jax.ShapeDtypeStruct((REACH * tok, heads * 2 * HD), BF16),
        jax.ShapeDtypeStruct((heads, 2, HD), F32),
    )
    return pl.pallas_call(
        attend_kernel,
        grid=(heads,),
        in_specs=[
            pl.BlockSpec(memory_space=pltpu.SMEM),
            pl.BlockSpec((tiles, LANES), lambda h: (0, 0)),
            vec,
            vec,
            at(group, first),
            at(group, first),
            at(HD, first),
            at(HD, first),
            at(2 * HD, 0),
            at(2 * HD, 0),
            at(2 * HD, 0),
        ],
        out_specs=(
            at(group, 0),
            at(2 * HD, 0),
            pl.BlockSpec((REACH * tok, 2 * HD), lambda h: (0, h)),
            pl.BlockSpec((1, 2, HD), lambda h: (h, 0, 0)),
        ),
        out_shape=out_shape,
        scratch_shapes=[
            pltpu.VMEM((tiles, span, LANES), F32),
            pltpu.VMEM((span, HD), BF16),
            pltpu.VMEM((span, HD), BF16),
            pltpu.VMEM((span, HD), BF16),
            pltpu.VMEM((span, HD), BF16),
            pltpu.VMEM((span, HD), F32),
            pltpu.VMEM((span, HD), F32),
        ],
        compiler_params=pltpu.CompilerParams(vmem_limit_bytes=40 * 2**20),
        cost_estimate=pl.CostEstimate(
            flops=heads * 8 * 256 * 576 * 128 * 10, bytes_accessed=heads * 2**21, transcendentals=0
        ),
    )(info, dstart, kscale, vscale, q, g, k_own, v_own, far, near_a, near_b)


def total_over_devices(value):
    size = lax.axis_size("seq")
    for bit in (1, 2, 4, 8, 16, 32):
        value = value + lax.ppermute(value, "seq", [(i, i ^ bit) for i in range(size)])
    for bit in (1, 2):
        value = value + lax.ppermute(value, "grp", [(i, i ^ bit) for i in range(4)])
    return value


def body(queries, key_base, value_base, out_grad, doc_lengths, key_scale, value_scale):
    tok = queries.shape[1]
    size = lax.axis_size("seq")
    heads = key_base.shape[2] // HD
    k_own = key_base[0]
    v_own = value_base[0]
    to_odd = [(i, i + 1) for i in range(0, size, 2)]
    to_even = [(i + 1, i) for i in range(0, size, 2)]
    forward = [(i, i + 2) for i in range(size - 2)]
    backward = [(i + 2, i) for i in range(size - 2)]
    device_pos = lax.axis_index("seq")
    parity = device_pos % 2

    mine = jnp.stack([k_own.reshape(tok, heads, HD), v_own.reshape(tok, heads, HD)], axis=2)
    mine = mine.reshape(tok, heads * 2 * HD)
    far = lax.ppermute(mine, "seq", forward)
    near_a = lax.ppermute(mine, "seq", to_odd)
    near_b = lax.ppermute(far, "seq", to_even)

    lengths = doc_lengths[0]
    starts = jnp.cumsum(lengths) - lengths
    first_key = (device_pos - REACH) * tok
    q_pos = device_pos * tok + jnp.arange(tok, dtype=jnp.int32)
    doc_start = jnp.max(jnp.where(starts[None, :] <= q_pos[:, None], starts[None, :], 0), axis=1)
    rel = (doc_start - first_key).reshape(tok // QT, QT)
    ends = REACH * tok + (jnp.arange(tok // QT, dtype=jnp.int32) + 1) * QT
    units = jnp.clip((ends - rel[:, 0] + KG - 1) // KG, 1, (DOC_MOST + QT) // KG)
    info = jnp.concatenate([units, parity[None]]).astype(jnp.int32)
    dstart = jnp.tile(rel, (1, LANES // QT))

    dq, own, part, sums = attend(
        heads, 0, info, dstart, key_scale[None], value_scale[None], queries[0], out_grad[0],
        k_own, v_own, far, near_a, near_b,
    )
    totals = total_over_devices(sums)
    two_back = part[:tok]
    one_back = part[tok:]
    from_odd = lax.ppermute(one_back, "seq", to_even)
    to_prev = lax.ppermute(two_back, "seq", backward)
    even_to_odd = lax.ppermute(one_back, "seq", [(i + 1, i) for i in range(1, size - 1, 2)])
    own = own + from_odd.astype(F32) + to_prev.astype(F32) + even_to_odd.astype(F32)
    own = own.reshape(tok, heads, 2, HD)
    grad_key_base = (own[:, :, 0].reshape(tok, heads * HD) * key_scale).astype(BF16)
    grad_value_base = (own[:, :, 1].reshape(tok, heads * HD) * value_scale).astype(BF16)
    norm = math.sqrt(lax.axis_size("grp") * size * tok)
    return (
        dq[None],
        grad_key_base[None],
        grad_value_base[None],
        totals[:, 0].reshape(heads * HD) / norm,
        totals[:, 1].reshape(heads * HD) / norm,
    )


def solution(mesh):
    return jax.shard_map(
        body,
        mesh=mesh,
        in_specs=(
            P("grp", "seq", None),
            P("grp", "seq", None),
            P("grp", "seq", None),
            P("grp", "seq", None),
            P("grp", None),
            P(),
            P(),
        ),
        out_specs=(P("grp", "seq", None), P("grp", "seq", None), P("grp", "seq", None), P(), P()),
        check_vma=False,
    )
```

profile of v0, /device:TPU:32, one launch (start us, length us, event | category | flops | bytes accessed | tf_op | source)
XLA Modules:
  0.0 117.4 jit_solution(5067497939252447030)
XLA Ops:
  0.7 2.8 %stack_reshape_squeeze.8 = bf16[256,4,1,128]{3,2,1,0:T(2,128)(2,1)} reshape(bf16[1,256,512]{2,1,0:T(8,128)(2,1)} %param.8) | data formatting | bytes 524288 | tf_op jit(solution)/shard_map/stack;reshape;squeeze | solution.py:190
  3.5 2.7 %stack_reshape_squeeze.9 = bf16[256,4,1,128]{3,2,1,0:T(2,128)(2,1)} reshape(bf16[1,256,512]{2,1,0:T(8,128)(2,1)} %param.9) | data formatting | bytes 524288 | tf_op jit(solution)/shard_map/stack;reshape;squeeze | solution.py:190
  6.2 2.3 %pad_maximum_fusion = bf16[256,4,2,128]{3,2,1,0:T(2,128)(2,1)S(1)} fusion(bf16[256,4,1,128]{3,2,1,0:T(2,128)(2,1)} %stack_reshape_squeeze.9, bf16[256,4,1,128]{3,2,1,0:T(2,128)(2,1)} %stack_reshape_squeeze.8), kind=kLoop, calls=%fused_computation.3 | loop fusion | flops 1048576 | bytes 1048576 | tf_op jit(solution)/shard_map/stack | solution.py:190
  9.6 1.8 %collective-permute-start.1 = (bf16[256,1024]{1,0:T(8,128)(2,1)}, bf16[256,1024]{1,0:T(8,128)(2,1)S(1)}, u32[]{:S(2)}, u32[]{:S(2)}) collective-permute-start(bf16[256,1024]{1,0:T(8,128)(2,1)} %reshape.112), channel_id=1, source_target_pairs={{0,1},{2,3},{4,5},{6,7},{8,9},{10,11},{12,13},{14,15},{16,17},{18,... | collective-permute-start | bytes 1572872 | tf_op jit(solution)/shard_map/ppermute | solution.py:193
  11.4 3.5 %collective-permute-start = (bf16[256,1024]{1,0:T(8,128)(2,1)}, bf16[256,1024]{1,0:T(8,128)(2,1)}, u32[]{:S(2)}, u32[]{:S(2)}) collective-permute-start(bf16[256,1024]{1,0:T(8,128)(2,1)} %reshape.112), channel_id=1, source_target_pairs={{0,2},{1,3},{2,4},{3,5},{4,6},{5,7},{6,8},{7,9},{8,10},{9,11},{10,... | collective-permute-start | bytes 1572872 | tf_op jit(solution)/shard_map/ppermute | solution.py:192
  15.4 13.5 %collective-permute-done.far = bf16[256,1024]{1,0:T(8,128)(2,1)} collective-permute-done((bf16[256,1024]{1,0:T(8,128)(2,1)}, bf16[256,1024]{1,0:T(8,128)(2,1)}, u32[]{:S(2)}, u32[]{:S(2)}) %collective-permute-start) | collective-permute-done | bytes 524320 | tf_op jit(solution)/shard_map/ppermute | solution.py:192
  28.9 1.5 %collective-permute-start.2 = (bf16[256,1024]{1,0:T(8,128)(2,1)}, bf16[256,1024]{1,0:T(8,128)(2,1)}, u32[]{:S(2)}, u32[]{:S(2)}) collective-permute-start(bf16[256,1024]{1,0:T(8,128)(2,1)} %collective-permute-done.far), channel_id=1, source_target_pairs={{1,0},{3,2},{5,4},{7,6},{9,8},{11,10},{13,12},{15,14},{17,16},{19,... | collective-permute-start | bytes 1572872 | tf_op jit(solution)/shard_map/ppermute | solution.py:194
  30.6 2.4 %collective-permute-done.2.near_b = bf16[256,1024]{1,0:T(8,128)(2,1)} collective-permute-done((bf16[256,1024]{1,0:T(8,128)(2,1)}, bf16[256,1024]{1,0:T(8,128)(2,1)}, u32[]{:S(2)}, u32[]{:S(2)}) %collective-permute-start.2) | collective-permute-done | bytes 524320 | tf_op jit(solution)/shard_map/ppermute | solution.py:194
  33.1 1.6 %copy-done.5 = bf16[1,256,4096]{2,1,0:T(8,128)(2,1)S(1)} copy-done((bf16[1,256,4096]{2,1,0:T(8,128)(2,1)S(1)}, bf16[1,256,4096]{2,1,0:T(8,128)(2,1)}, u32[]{:S(2)}) %copy-start.5) | copy-done | bytes 2097176
  34.6 20.2 %shard_map.110 = (bf16[256,4096]{1,0:T(8,128)(2,1)}, f32[256,1024]{1,0:T(8,128)S(1)}, bf16[512,1024]{1,0:T(8,128)(2,1)S(1)}, f32[4,2,128]{2,1,0:T(2,128)S(1)}) custom-call(s32[3]{0:T(128)S(1)} %pad_add_fusion.info, s32[2,256]{1,0:T(2,128)S(1)} %bitcast.23, f32[1,512]{1,0:T(1,128)S(1)} %bitcast.21, f32[1,512]{1,0:T(1,128)S(1)} %bitcast.22, ...), custom_call_target="tpu_custom_call" | custom-call | flops 6039797760 | bytes 8388608 | tf_op jit(solution)/shard_map/pallas_call | solution.py:129
  54.9 6.4 %collective-permute-start.4 = (bf16[256,1024]{1,0:T(8,128)(2,1)S(1)}, bf16[256,1024]{1,0:T(8,128)(2,1)S(1)}, u32[]{:S(2)}, u32[]{:S(2)}) collective-permute-start(bf16[256,1024]{1,0:T(8,128)(2,1)S(1)} %get-tuple-element.15), channel_id=1, source_target_pairs={{2,0},{3,1},{4,2},{5,3},{6,4},{7,5},{8,6},{9,7},{10,8},{11,9},{12,... | collective-permute-start | bytes 1572872 | tf_op jit(solution)/shard_map/ppermute | solution.py:215
  61.3 2.2 %collective-permute-start.5 = (bf16[256,1024]{1,0:T(8,128)(2,1)S(1)}, bf16[256,1024]{1,0:T(8,128)(2,1)S(1)}, u32[]{:S(2)}, u32[]{:S(2)}) collective-permute-start(bf16[256,1024]{1,0:T(8,128)(2,1)S(1)} %get-tuple-element.16), channel_id=1, source_target_pairs={{2,1},{4,3},{6,5},{8,7},{10,9},{12,11},{14,13},{16,15},{18,17},{20... | collective-permute-start | bytes 1572872 | tf_op jit(solution)/shard_map/ppermute | solution.py:216
  63.5 1.3 %collective-permute-start.3 = (bf16[256,1024]{1,0:T(8,128)(2,1)S(1)}, bf16[256,1024]{1,0:T(8,128)(2,1)S(1)}, u32[]{:S(2)}, u32[]{:S(2)}) collective-permute-start(bf16[256,1024]{1,0:T(8,128)(2,1)S(1)} %get-tuple-element.16), channel_id=1, source_target_pairs={{1,0},{3,2},{5,4},{7,6},{9,8},{11,10},{13,12},{15,14},{17,16},{19,... | collective-permute-start | bytes 1572872 | tf_op jit(solution)/shard_map/ppermute | solution.py:214
  67.4 1.3 %collective-permute-start.7 = (f32[4,2,128]{2,1,0:T(2,128)S(1)}, f32[4,2,128]{2,1,0:T(2,128)S(1)}, u32[]{:S(2)}, u32[]{:S(2)}) collective-permute-start(f32[4,2,128]{2,1,0:T(2,128)S(1)} %add.67), channel_id=1, source_target_pairs={{0,2},{1,3},{2,0},{3,1},{4,6},{5,7},{6,4},{7,5},{8,10},{9,11},{10,... | collective-permute-start | bytes 12296 | tf_op jit(solution)/shard_map/ppermute | solution.py:171
  68.7 8.6 %collective-permute-done.7 = f32[4,2,128]{2,1,0:T(2,128)S(1)} collective-permute-done((f32[4,2,128]{2,1,0:T(2,128)S(1)}, f32[4,2,128]{2,1,0:T(2,128)S(1)}, u32[]{:S(2)}, u32[]{:S(2)}) %collective-permute-start.7) | collective-permute-done | bytes 4128 | tf_op jit(solution)/shard_map/ppermute | solution.py:171
  77.3 5.1 %collective-permute-done.8 = f32[4,2,128]{2,1,0:T(2,128)S(1)} collective-permute-done((f32[4,2,128]{2,1,0:T(2,128)S(1)}, f32[4,2,128]{2,1,0:T(2,128)S(1)}, u32[]{:S(2)}, u32[]{:S(2)}) %collective-permute-start.8) | collective-permute-done | bytes 4128 | tf_op jit(solution)/shard_map/ppermute | solution.py:171
  83.4 2.6 %collective-permute-done.9 = f32[4,2,128]{2,1,0:T(2,128)S(1)} collective-permute-done((f32[4,2,128]{2,1,0:T(2,128)S(1)}, f32[4,2,128]{2,1,0:T(2,128)S(1)}, u32[]{:S(2)}, u32[]{:S(2)}) %collective-permute-start.9) | collective-permute-done | bytes 4128 | tf_op jit(solution)/shard_map/ppermute | solution.py:171
  86.0 5.1 %collective-permute-start.10 = (f32[4,2,128]{2,1,0:T(2,128)S(1)}, f32[4,2,128]{2,1,0:T(2,128)S(1)}, u32[]{:S(2)}, u32[]{:S(2)}) collective-permute-start(f32[4,2,128]{2,1,0:T(2,128)S(1)} %add.70), channel_id=1, source_target_pairs={{0,16},{1,17},{2,18},{3,19},{4,20},{5,21},{6,22},{7,23},{8,24},{9,... | collective-permute-start | bytes 12296 | tf_op jit(solution)/shard_map/ppermute | solution.py:171
  91.1 1.6 %collective-permute-done.10 = f32[4,2,128]{2,1,0:T(2,128)S(1)} collective-permute-done((f32[4,2,128]{2,1,0:T(2,128)S(1)}, f32[4,2,128]{2,1,0:T(2,128)S(1)}, u32[]{:S(2)}, u32[]{:S(2)}) %collective-permute-start.10) | collective-permute-done | bytes 4128 | tf_op jit(solution)/shard_map/ppermute | solution.py:171
  92.7 8.2 %collective-permute-start.11 = (f32[4,2,128]{2,1,0:T(2,128)S(1)}, f32[4,2,128]{2,1,0:T(2,128)S(1)}, u32[]{:S(2)}, u32[]{:S(2)}) collective-permute-start(f32[4,2,128]{2,1,0:T(2,128)S(1)} %add.71), channel_id=1, source_target_pairs={{0,32},{1,33},{2,34},{3,35},{4,36},{5,37},{6,38},{7,39},{8,40},{9,... | collective-permute-start | bytes 12296 | tf_op jit(solution)/shard_map/ppermute | solution.py:171
  100.9 1.6 %collective-permute-done.11 = f32[4,2,128]{2,1,0:T(2,128)S(1)} collective-permute-done((f32[4,2,128]{2,1,0:T(2,128)S(1)}, f32[4,2,128]{2,1,0:T(2,128)S(1)}, u32[]{:S(2)}, u32[]{:S(2)}) %collective-permute-start.11) | collective-permute-done | bytes 4128 | tf_op jit(solution)/shard_map/ppermute | solution.py:171
  102.9 3.2 %collective-permute-done.12 = f32[4,2,128]{2,1,0:T(2,128)S(1)} collective-permute-done((f32[4,2,128]{2,1,0:T(2,128)S(1)}, f32[4,2,128]{2,1,0:T(2,128)S(1)}, u32[]{:S(2)}, u32[]{:S(2)}) %collective-permute-start.12) | collective-permute-done | bytes 4128 | tf_op jit(solution)/shard_map/ppermute | solution.py:173
  106.7 4.6 %collective-permute-done.13 = f32[4,2,128]{2,1,0:T(2,128)S(1)} collective-permute-done((f32[4,2,128]{2,1,0:T(2,128)S(1)}, f32[4,2,128]{2,1,0:T(2,128)S(1)}, u32[]{:S(2)}, u32[]{:S(2)}) %collective-permute-start.13) | collective-permute-done | bytes 4128 | tf_op jit(solution)/shard_map/ppermute | solution.py:173
  113.1 3.0 %slice_reduce_fusion = (f32[256,4,128]{2,1,0:T(4,128)S(1)}, f32[256,4,128]{2,1,0:T(4,128)S(1)}) fusion(f32[256,4,2,128]{3,2,1,0:T(2,128)S(1)} %reshape.113), kind=kLoop, calls=%fused_computation.1 | loop fusion | bytes 2097152 | tf_op jit(solution)/shard_map/slice | solution.py:220
  (49 shorter events, 9.7 us)
Async XLA Ops:
  0.6 32.4 %copy-start = (bf16[1,256,512]{2,1,0:T(8,128)(2,1)S(1)}, bf16[1,256,512]{2,1,0:T(8,128)(2,1)}, u32[]{:S(2)}) copy-start(bf16[1,256,512]{2,1,0:T(8,128)(2,1)} %param.8) | copy-start | bytes 786436
  0.6 32.4 %copy-start.1 = (bf16[1,256,512]{2,1,0:T(8,128)(2,1)S(1)}, bf16[1,256,512]{2,1,0:T(8,128)(2,1)}, u32[]{:S(2)}) copy-start(bf16[1,256,512]{2,1,0:T(8,128)(2,1)} %param.9) | copy-start | bytes 786436
  0.7 14.2 %copy-start.6 = (s32[1,128]{1,0:T(1,128)S(1)}, s32[1,128]{1,0:T(1,128)}, u32[]{:S(2)}) copy-start(s32[1,128]{1,0:T(1,128)} %param.11) | copy-start | bytes 1540
  0.7 32.4 %copy-start.2 = (f32[512]{0:T(512)S(1)}, f32[512]{0:T(512)}, u32[]{:S(2)}) copy-start(f32[512]{0:T(512)} %param.12) | copy-start | bytes 6148
  0.7 32.4 %copy-start.3 = (f32[512]{0:T(512)S(1)}, f32[512]{0:T(512)}, u32[]{:S(2)}) copy-start(f32[512]{0:T(512)} %param.13) | copy-start | bytes 6148
  0.7 32.4 %copy-start.4 = (bf16[1,256,4096]{2,1,0:T(8,128)(2,1)S(1)}, bf16[1,256,4096]{2,1,0:T(8,128)(2,1)}, u32[]{:S(2)}) copy-start(bf16[1,256,4096]{2,1,0:T(8,128)(2,1)} %param.7) | copy-start | bytes 6291460
  9.6 21.0 %collective-permute-start.1 = (bf16[256,1024]{1,0:T(8,128)(2,1)}, bf16[256,1024]{1,0:T(8,128)(2,1)S(1)}, u32[]{:S(2)}, u32[]{:S(2)}) collective-permute-start(bf16[256,1024]{1,0:T(8,128)(2,1)} %reshape.112), channel_id=1, source_target_pairs={{0,1},{2,3},{4,5},{6,7},{8,9},{10,11},{12,13},{14,15},{16,17},{18,... | collective-permute-start | bytes 1572872 | tf_op jit(solution)/shard_map/ppermute | solution.py:193
  11.4 17.5 %collective-permute-start = (bf16[256,1024]{1,0:T(8,128)(2,1)}, bf16[256,1024]{1,0:T(8,128)(2,1)}, u32[]{:S(2)}, u32[]{:S(2)}) collective-permute-start(bf16[256,1024]{1,0:T(8,128)(2,1)} %reshape.112), channel_id=1, source_target_pairs={{0,2},{1,3},{2,4},{3,5},{4,6},{5,7},{6,8},{7,9},{8,10},{9,11},{10,... | collective-permute-start | bytes 1572872 | tf_op jit(solution)/shard_map/ppermute | solution.py:192
  28.9 4.1 %collective-permute-start.2 = (bf16[256,1024]{1,0:T(8,128)(2,1)}, bf16[256,1024]{1,0:T(8,128)(2,1)}, u32[]{:S(2)}, u32[]{:S(2)}) collective-permute-start(bf16[256,1024]{1,0:T(8,128)(2,1)} %collective-permute-done.far), channel_id=1, source_target_pairs={{1,0},{3,2},{5,4},{7,6},{9,8},{11,10},{13,12},{15,14},{17,16},{19,... | collective-permute-start | bytes 1572872 | tf_op jit(solution)/shard_map/ppermute | solution.py:194
  33.0 1.6 %copy-start.5 = (bf16[1,256,4096]{2,1,0:T(8,128)(2,1)S(1)}, bf16[1,256,4096]{2,1,0:T(8,128)(2,1)}, u32[]{:S(2)}) copy-start(bf16[1,256,4096]{2,1,0:T(8,128)(2,1)} %param.10) | copy-start | bytes 6291460
  54.9 57.0 %collective-permute-start.4 = (bf16[256,1024]{1,0:T(8,128)(2,1)S(1)}, bf16[256,1024]{1,0:T(8,128)(2,1)S(1)}, u32[]{:S(2)}, u32[]{:S(2)}) collective-permute-start(bf16[256,1024]{1,0:T(8,128)(2,1)S(1)} %get-tuple-element.15), channel_id=1, source_target_pairs={{2,0},{3,1},{4,2},{5,3},{6,4},{7,5},{8,6},{9,7},{10,8},{11,9},{12,... | collective-permute-start | bytes 1572872 | tf_op jit(solution)/shard_map/ppermute | solution.py:215
  61.3 50.5 %collective-permute-start.5 = (bf16[256,1024]{1,0:T(8,128)(2,1)S(1)}, bf16[256,1024]{1,0:T(8,128)(2,1)S(1)}, u32[]{:S(2)}, u32[]{:S(2)}) collective-permute-start(bf16[256,1024]{1,0:T(8,128)(2,1)S(1)} %get-tuple-element.16), channel_id=1, source_target_pairs={{2,1},{4,3},{6,5},{8,7},{10,9},{12,11},{14,13},{16,15},{18,17},{20... | collective-permute-start | bytes 1572872 | tf_op jit(solution)/shard_map/ppermute | solution.py:216
  63.5 48.3 %collective-permute-start.3 = (bf16[256,1024]{1,0:T(8,128)(2,1)S(1)}, bf16[256,1024]{1,0:T(8,128)(2,1)S(1)}, u32[]{:S(2)}, u32[]{:S(2)}) collective-permute-start(bf16[256,1024]{1,0:T(8,128)(2,1)S(1)} %get-tuple-element.16), channel_id=1, source_target_pairs={{1,0},{3,2},{5,4},{7,6},{9,8},{11,10},{13,12},{15,14},{17,16},{19,... | collective-permute-start | bytes 1572872 | tf_op jit(solution)/shard_map/ppermute | solution.py:214
  64.8 2.5 %collective-permute-start.6 = (f32[4,2,128]{2,1,0:T(2,128)S(1)}, f32[4,2,128]{2,1,0:T(2,128)S(1)}, u32[]{:S(2)}, u32[]{:S(2)}) collective-permute-start(f32[4,2,128]{2,1,0:T(2,128)S(1)} %get-tuple-element.12), channel_id=1, source_target_pairs={{0,1},{1,0},{2,3},{3,2},{4,5},{5,4},{6,7},{7,6},{8,9},{9,8},{10,11... | collective-permute-start | bytes 12296 | tf_op jit(solution)/shard_map/ppermute | solution.py:171
  67.4 9.9 %collective-permute-start.7 = (f32[4,2,128]{2,1,0:T(2,128)S(1)}, f32[4,2,128]{2,1,0:T(2,128)S(1)}, u32[]{:S(2)}, u32[]{:S(2)}) collective-permute-start(f32[4,2,128]{2,1,0:T(2,128)S(1)} %add.67), channel_id=1, source_target_pairs={{0,2},{1,3},{2,0},{3,1},{4,6},{5,7},{6,4},{7,5},{8,10},{9,11},{10,... | collective-permute-start | bytes 12296 | tf_op jit(solution)/shard_map/ppermute | solution.py:171
  77.3 5.1 %collective-permute-start.8 = (f32[4,2,128]{2,1,0:T(2,128)S(1)}, f32[4,2,128]{2,1,0:T(2,128)S(1)}, u32[]{:S(2)}, u32[]{:S(2)}) collective-permute-start(f32[4,2,128]{2,1,0:T(2,128)S(1)} %add.68), channel_id=1, source_target_pairs={{0,4},{1,5},{2,6},{3,7},{4,0},{5,1},{6,2},{7,3},{8,12},{9,13},{10,... | collective-permute-start | bytes 12296 | tf_op jit(solution)/shard_map/ppermute | solution.py:171
  82.4 3.6 %collective-permute-start.9 = (f32[4,2,128]{2,1,0:T(2,128)S(1)}, f32[4,2,128]{2,1,0:T(2,128)S(1)}, u32[]{:S(2)}, u32[]{:S(2)}) collective-permute-start(f32[4,2,128]{2,1,0:T(2,128)S(1)} %add.69), channel_id=1, source_target_pairs={{0,8},{1,9},{2,10},{3,11},{4,12},{5,13},{6,14},{7,15},{8,0},{9,1},... | collective-permute-start | bytes 12296 | tf_op jit(solution)/shard_map/ppermute | solution.py:171
  86.0 6.7 %collective-permute-start.10 = (f32[4,2,128]{2,1,0:T(2,128)S(1)}, f32[4,2,128]{2,1,0:T(2,128)S(1)}, u32[]{:S(2)}, u32[]{:S(2)}) collective-permute-start(f32[4,2,128]{2,1,0:T(2,128)S(1)} %add.70), channel_id=1, source_target_pairs={{0,16},{1,17},{2,18},{3,19},{4,20},{5,21},{6,22},{7,23},{8,24},{9,... | collective-permute-start | bytes 12296 | tf_op jit(solution)/shard_map/ppermute | solution.py:171
  92.7 9.8 %collective-permute-start.11 = (f32[4,2,128]{2,1,0:T(2,128)S(1)}, f32[4,2,128]{2,1,0:T(2,128)S(1)}, u32[]{:S(2)}, u32[]{:S(2)}) collective-permute-start(f32[4,2,128]{2,1,0:T(2,128)S(1)} %add.71), channel_id=1, source_target_pairs={{0,32},{1,33},{2,34},{3,35},{4,36},{5,37},{6,38},{7,39},{8,40},{9,... | collective-permute-start | bytes 12296 | tf_op jit(solution)/shard_map/ppermute | solution.py:171
  102.5 3.6 %collective-permute-start.12 = (f32[4,2,128]{2,1,0:T(2,128)S(1)}, f32[4,2,128]{2,1,0:T(2,128)S(1)}, u32[]{:S(2)}, u32[]{:S(2)}) collective-permute-start(f32[4,2,128]{2,1,0:T(2,128)S(1)} %add.72), channel_id=1, source_target_pairs={{0,64},{64,0},{128,192},{192,128},{1,65},{65,1},{129,193},{193,129... | collective-permute-start | bytes 12296 | tf_op jit(solution)/shard_map/ppermute | solution.py:173
  106.1 5.1 %collective-permute-start.13 = (f32[4,2,128]{2,1,0:T(2,128)S(1)}, f32[4,2,128]{2,1,0:T(2,128)S(1)}, u32[]{:S(2)}, u32[]{:S(2)}) collective-permute-start(f32[4,2,128]{2,1,0:T(2,128)S(1)} %add.73), channel_id=1, source_target_pairs={{0,128},{64,192},{128,0},{192,64},{1,129},{65,193},{129,1},{193,65... | collective-permute-start | bytes 12296 | tf_op jit(solution)/shard_map/ppermute | solution.py:173
where the time goes:
time: 118 us; the launch traced here: 117 us
  waiting for transfers between devices  44.4 us (38%)
  starting transfers between devices  34.5 us (29%)
  Pallas kernels  20.2 us (17%)
  local copies, waits for them, and re-layouts  12.7 us (11%)
  other arithmetic  4.76 us (4%)
    ppermute x6, waiting for transfers between devices, total_over_devices(): lax.ppermute(value, 'seq', [(i, i ^ bit) for i in range(size)])  20.7 us
    pallas_call x1, Pallas kernels, attend(): pl.pallas_call(attend_kernel, grid=(heads,), in_specs=[pl.BlockSpec(memor...  20.2 us
    ppermute x6, starting transfers between devices, total_over_devices(): lax.ppermute(value, 'seq', [(i, i ^ bit) for i in range(size)])  16.9 us
    ppermute x1, waiting for transfers between devices, body(): far = lax.ppermute(mine, 'seq', forward)  13.5 us
    ppermute x2, waiting for transfers between devices, total_over_devices(): value = value + lax.ppermute(value, 'grp', [(i, i ^ bit) for i in range(4)])  7.78 us
    ppermute x1, starting transfers between devices, body(): to_prev = lax.ppermute(two_back, 'seq', backward)  6.44 us
    another operation x2, local copies, waits for them, and re-layouts, body(): jnp.stack([k_own.reshape(tok, heads, HD), v_own.reshape(tok, heads, HD)],...  5.46 us
    ppermute x1, starting transfers between devices, body(): far = lax.ppermute(mine, 'seq', forward)  3.49 us
  transfers between devices with their start and end apart: 14, of which 10 were waited for; matrix products, arithmetic and copies ran while one was open for 1% of the time, Pallas kernels for 0%

commit v1 on v0

v1 whole, which is shorter than its diff:
```python
import functools
import math

import jax
import jax.numpy as jnp
from jax import lax
from jax.experimental import pallas as pl
from jax.experimental.pallas import tpu as pltpu
from jax.sharding import PartitionSpec as P

HD = 128
REACH = 2
DOC_MOST = 512
QT = 64
KG = 64
LANES = 256
HEADS_STEP = 2
NEG = -1e30
F32 = jnp.float32
BF16 = jnp.bfloat16
NT = (((1,), (1,)), ((), ()))


def attend_kernel(
    info, dstart, kscale, vscale, q_ref, g_ref, k_own, v_own,
    far_k, far_v, near_ka, near_va, near_kb, near_vb,
    dq_ref, own_ref, two_ref, one_ref, sums_ref,
    bias, k_raw, v_raw, k_win, v_win, dk_acc, dv_acc,
):
    tok, width = k_own.shape
    heads = width // HD
    front = REACH * tok
    per_group = q_ref.shape[1] // width
    packed = LANES // QT
    parts = per_group // packed
    tiles = tok // QT
    most = (DOC_MOST + QT) // KG
    inv_root = 1.0 / math.sqrt(HD)
    log2_scale = inv_root * math.log2(math.e)

    @pl.when(pl.program_id(0) == 0)
    def _():
        reach = front + QT
        k_pos = lax.broadcasted_iota(jnp.int32, (reach, LANES), 0)
        lane = lax.broadcasted_iota(jnp.int32, (reach, LANES), 1) % QT
        for tile in range(tiles):
            start = dstart[tile : tile + 1, :] - tile * QT
            ok = (k_pos >= start) & (k_pos <= lane + front)
            bias[tile] = jnp.where(ok, 0.0, NEG)

    even = info[tiles] == 0
    for head in range(heads):
        cols = slice(head * HD, (head + 1) * HD)
        k_raw[head, :tok] = far_k[:, cols]
        v_raw[head, :tok] = far_v[:, cols]
        k_raw[head, tok:front] = jnp.where(even, near_kb[:, cols], near_ka[:, cols])
        v_raw[head, tok:front] = jnp.where(even, near_vb[:, cols], near_va[:, cols])
        k_raw[head, front:] = k_own[:, cols]
        v_raw[head, front:] = v_own[:, cols]
        k_win[head] = (k_raw[head].astype(F32) * kscale[:, cols]).astype(BF16)
        v_win[head] = (v_raw[head].astype(F32) * vscale[:, cols]).astype(BF16)
    dk_acc[...] = jnp.zeros_like(dk_acc)
    dv_acc[...] = jnp.zeros_like(dv_acc)

    def one_tile(tile, units):
        row = pl.multiple_of(tile * QT, QT)
        count = units * KG
        low = pl.multiple_of(front + (tile + 1) * QT - count, KG)
        rows = pl.ds(low, count)
        mask = bias[tile, front + QT - count :, :]

        def begin(group):
            head = group // parts
            at = range(group * packed, (group + 1) * packed)
            cols = [slice(c * HD, (c + 1) * HD) for c in at]
            q_part = jnp.concatenate([q_ref[pl.ds(row, QT), c] for c in cols], axis=0)
            g_part = jnp.concatenate([g_ref[pl.ds(row, QT), c] for c in cols], axis=0)
            scores = lax.dot_general(k_win[head, rows, :], q_part, NT, preferred_element_type=F32)
            dprobs = lax.dot_general(v_win[head, rows, :], g_part, NT, preferred_element_type=F32)
            return q_part, g_part, scores, dprobs

        def middle(q_part, g_part, scores, dprobs):
            scores = scores * log2_scale + mask
            peak = jnp.max(scores, axis=0, keepdims=True)
            raised = jnp.exp2(scores - peak)
            inverse = 1.0 / jnp.sum(raised, axis=0, keepdims=True)
            delta = jnp.sum(raised * dprobs, axis=0, keepdims=True) * inverse
            weights = raised * inverse
            probs = weights.astype(BF16)
            dscores = (weights * (dprobs - delta)).astype(BF16)
            return q_part, g_part, probs, dscores

        totals = [None] * heads

        def finish(group, q_part, g_part, probs, dscores):
            head = group // parts
            dv = jnp.dot(probs, g_part, preferred_element_type=F32)
            dk = jnp.dot(dscores, q_part, preferred_element_type=F32)
            if totals[head] is not None:
                dk = dk + totals[head][0]
                dv = dv + totals[head][1]
            totals[head] = (dk, dv)
            keys_t = k_win[head, rows, :].T
            dq_t = jnp.dot(keys_t, dscores, preferred_element_type=F32) * inv_root
            dq = dq_t.T.astype(BF16)
            for i in range(packed):
                c = (group * packed + i) * HD
                dq_ref[pl.ds(row, QT), c : c + HD] = dq[i * QT : (i + 1) * QT]
            if group % parts == parts - 1:
                dk_acc[head, rows, :] += dk
                dv_acc[head, rows, :] += dv

        groups = heads * parts
        begun = begin(0)
        done = None
        for group in range(groups):
            following = begin(group + 1) if group + 1 < groups else None
            middle_out = middle(*begun)
            if done is not None:
                finish(group - 1, *done)
            done = middle_out
            begun = following
        finish(groups - 1, *done)

    def tile_step(tile, carry):
        units = info[tile]
        for static in range(1, most + 1):
            pl.when(units == static)(functools.partial(one_tile, tile, static))
        return carry

    lax.fori_loop(0, tiles, tile_step, 0)
    for head in range(heads):
        cols = slice(head * HD, (head + 1) * HD)
        dk = dk_acc[head] * inv_root
        dv = dv_acc[head]
        own_ref[0, :, cols] = dk[front:]
        own_ref[1, :, cols] = dv[front:]
        two_ref[0, :, cols] = dk[:tok].astype(BF16)
        two_ref[1, :, cols] = dv[:tok].astype(BF16)
        one_ref[0, :, cols] = dk[tok:front].astype(BF16)
        one_ref[1, :, cols] = dv[tok:front].astype(BF16)
        k_sum = jnp.sum(dk * k_raw[head].astype(F32), axis=0, keepdims=True)
        v_sum = jnp.sum(dv * v_raw[head].astype(F32), axis=0, keepdims=True)
        for copy in range(sums_ref.shape[0]):
            sums_ref[copy, head, 0:1, :] = k_sum
            sums_ref[copy, head, 1:2, :] = v_sum


def attend(info, dstart, kscale, vscale, q, g, k_own, v_own, *received):
    tok, width = k_own.shape
    span = (REACH + 1) * tok
    tiles = tok // QT
    heads = width // HD
    step = HEADS_STEP * HD

    def at(columns):
        return pl.BlockSpec((tok, columns), lambda h: (0, h))

    pair = pl.BlockSpec((2, tok, step), lambda h: (0, 0, h))
    vec = pl.BlockSpec((1, step), lambda h: (0, h))
    group = at(q.shape[1] * step // width)
    out_shape = (
        jax.ShapeDtypeStruct(q.shape, BF16),
        jax.ShapeDtypeStruct((2, tok, width), F32),
        jax.ShapeDtypeStruct((2, tok, width), BF16),
        jax.ShapeDtypeStruct((2, tok, width), BF16),
        jax.ShapeDtypeStruct((8, heads, 2, HD), F32),
    )
    window = pltpu.VMEM((HEADS_STEP, span, HD), BF16)
    total = pltpu.VMEM((HEADS_STEP, span, HD), F32)
    return pl.pallas_call(
        attend_kernel,
        grid=(heads // HEADS_STEP,),
        in_specs=[
            pl.BlockSpec(memory_space=pltpu.SMEM),
            pl.BlockSpec((tiles, LANES), lambda h: (0, 0)),
            vec,
            vec,
            group,
            group,
        ]
        + [at(step)] * 8,
        out_specs=(
            group,
            pair,
            pair,
            pair,
            pl.BlockSpec((8, HEADS_STEP, 2, HD), lambda h: (0, h, 0, 0)),
        ),
        out_shape=out_shape,
        scratch_shapes=[
            pltpu.VMEM((tiles, REACH * tok + QT, LANES), F32),
            window,
            window,
            window,
            window,
            total,
            total,
        ],
        compiler_params=pltpu.CompilerParams(vmem_limit_bytes=58 * 2**20),
        cost_estimate=pl.CostEstimate(
            flops=heads * 8 * 256 * 576 * 128 * 10, bytes_accessed=heads * 2**21, transcendentals=0
        ),
    )(info, dstart, kscale, vscale, q, g, k_own, v_own, *received)


def finish_kernel(even_ref, kscale, vscale, own, swapped, back, gk_ref, gv_ref):
    even = even_ref[0] == 0
    for half, (out, scale) in enumerate(((gk_ref, kscale), (gv_ref, vscale))):
        near = jnp.where(even, swapped[half].astype(F32), 0.0)
        total = own[half] + near + back[half].astype(F32)
        out[...] = (total * scale[...]).astype(BF16)


def finish(parity, kscale, vscale, own, swapped, back):
    _, tok, width = own.shape
    step = 2 * HD
    pair = pl.BlockSpec((2, tok, step), lambda i: (0, 0, i))
    vec = pl.BlockSpec((1, step), lambda i: (0, i))
    out = pl.BlockSpec((tok, step), lambda i: (0, i))
    return pl.pallas_call(
        finish_kernel,
        grid=(width // step,),
        in_specs=[pl.BlockSpec(memory_space=pltpu.SMEM), vec, vec, pair, pair, pair],
        out_specs=(out, out),
        out_shape=(jax.ShapeDtypeStruct((tok, width), BF16),) * 2,
        compiler_params=pltpu.CompilerParams(vmem_limit_bytes=58 * 2**20),
    )(parity[None], kscale, vscale, own, swapped, back)


def spread_sum(copies, axis, groups):
    return jnp.sum(lax.all_to_all(copies, axis, 0, 0, axis_index_groups=groups), axis=0)


def repeated(value, count):
    return jnp.broadcast_to(value[None], (count,) + value.shape)


def body(queries, key_base, value_base, out_grad, doc_lengths, key_scale, value_scale):
    tok = queries.shape[1]
    size = lax.axis_size("seq")
    heads = key_base.shape[2] // HD
    group = queries.shape[2] // heads
    k_own = key_base[0]
    v_own = value_base[0]
    to_odd = [(i, i + 1) for i in range(0, size, 2)]
    to_even = [(i + 1, i) for i in range(0, size, 2)]
    forward = [(i, i + 2) for i in range(size - 2)]
    backward = [(i + 2, i) for i in range(size - 2)]
    device_pos = lax.axis_index("seq")
    parity = device_pos % 2

    far_k = lax.ppermute(k_own, "seq", forward)
    far_v = lax.ppermute(v_own, "seq", forward)
    near_ka = lax.ppermute(k_own, "seq", to_odd)
    near_va = lax.ppermute(v_own, "seq", to_odd)
    near_kb = lax.ppermute(far_k, "seq", to_even)
    near_vb = lax.ppermute(far_v, "seq", to_even)

    lengths = doc_lengths[0]
    starts = jnp.cumsum(lengths) - lengths
    first_key = (device_pos - REACH) * tok
    q_pos = device_pos * tok + jnp.arange(tok, dtype=jnp.int32)
    doc_start = jnp.max(jnp.where(starts[None, :] <= q_pos[:, None], starts[None, :], 0), axis=1)
    rel = (doc_start - first_key).reshape(tok // QT, QT)
    ends = REACH * tok + (jnp.arange(tok // QT, dtype=jnp.int32) + 1) * QT
    units = jnp.clip((ends - rel[:, 0] + KG - 1) // KG, 1, (DOC_MOST + QT) // KG)
    info = jnp.concatenate([units, parity[None]]).astype(jnp.int32)
    dstart = jnp.tile(rel, (1, LANES // QT))

    dq, own, two_back, one_back, sums = attend(
        info, dstart, key_scale[None], value_scale[None], queries[0], out_grad[0],
        k_own, v_own, far_k, far_v, near_ka, near_va, near_kb, near_vb,
    )
    rows = [[a * 8 + b for b in range(8)] for a in range(size // 8)]
    columns = [[a * 8 + b for a in range(size // 8)] for b in range(8)]
    partial = spread_sum(sums, "seq", rows)
    partial, one_back = lax.optimization_barrier((partial, one_back))
    swapped = lax.ppermute(one_back, "seq", to_odd + to_even)
    partial = spread_sum(repeated(partial, 4), "grp", None)
    partial, swapped = lax.optimization_barrier((partial, swapped))
    swapped_odd = jnp.where(parity == 1, swapped.astype(F32), 0.0)
    joined = (two_back.astype(F32) + swapped_odd).astype(BF16)
    back = lax.ppermute(joined, "seq", backward)
    partial, joined = lax.optimization_barrier((partial, joined))
    totals = spread_sum(repeated(partial, 8), "seq", columns)
    totals, back = lax.optimization_barrier((totals, back))
    grad_key_base, grad_value_base = finish(
        parity, key_scale[None], value_scale[None], own, swapped, back
    )
    norm = math.sqrt(lax.axis_size("grp") * size * tok)
    return (
        dq[None],
        grad_key_base[None],
        grad_value_base[None],
        totals[:, 0].reshape(heads * HD) / norm,
        totals[:, 1].reshape(heads * HD) / norm,
    )


def solution(mesh):
    return jax.shard_map(
        body,
        mesh=mesh,
        in_specs=(
            P("grp", "seq", None),
            P("grp", "seq", None),
            P("grp", "seq", None),
            P("grp", "seq", None),
            P("grp", None),
            P(),
            P(),
        ),
        out_specs=(P("grp", "seq", None), P("grp", "seq", None), P("grp", "seq", None), P(), P()),
        check_vma=False,
    )
```

time: 118 us -> 88.2 us (0.75)
  waiting for transfers between devices: 44.4 us -> 10.9 us
  blocking collectives: 0 us -> 33 us
  starting transfers between devices: 34.5 us -> 20.8 us
  local copies, waits for them, and re-layouts: 12.7 us -> 2.39 us
  Pallas kernels: 20.2 us -> 15.7 us
    ppermute x14 -> x8, waiting for transfers between devices: 44.4 us -> 5.58 us  [the longest x1 3.29 us: body(): far_v = lax.ppermute(v_own, 'seq', forward)]
    all_to_all x0 -> x2, blocking collectives: none -> 33 us  [spread_sum(): lax.all_to_all(copies, axis, 0, 0, axis_index_groups=groups)]
    ppermute x14 -> x8, starting transfers between devices: 34.5 us -> 16.2 us  [the longest x1 3.79 us: body(): back = lax.ppermute(joined, 'seq', backward)]
    all_to_all x0 -> x1, waiting for transfers between devices: none -> 5.36 us  [spread_sum(): lax.all_to_all(copies, axis, 0, 0, axis_index_groups=groups)]
    another operation x4 -> x2, local copies, waits for them, and re-layouts: 5.88 us -> 0.68 us  [body(): dstart = jnp.tile(rel, (1, LANES // QT))]
    all_to_all x0 -> x1, starting transfers between devices: none -> 4.58 us  [spread_sum(): lax.all_to_all(copies, axis, 0, 0, axis_index_groups=groups)]
    pallas_call x1 -> x2, Pallas kernels: 20.2 us -> 15.7 us  [the longest x1 13.4 us: attend(): pl.pallas_call(attend_kernel, grid=(heads // HEADS_STEP,), in_specs=[pl.B...]
    slice x2 -> x0, local copies, waits for them, and re-layouts: 3.04 us -> none  [the longest x1 2.97 us: body(): own[:, :, 1].reshape(tok, heads * HD) * value_scale]
  transfers between devices with their start and end apart: 14 -> 9, of which waited for: 10 -> 4; matrix products, arithmetic and copies ran while one was open for 1% -> 4% of each run, Pallas kernels for 0% -> 0%
where the time goes in v1:
time: 88.2 us
  blocking collectives  33 us (37%)
  starting transfers between devices  20.8 us (24%)
  Pallas kernels  15.7 us (18%)
  waiting for transfers between devices  10.9 us (12%)
  other arithmetic  4.5 us (5%)
  local copies, waits for them, and re-layouts  2.39 us (3%)
    all_to_all x2, blocking collectives, spread_sum(): lax.all_to_all(copies, axis, 0, 0, axis_index_groups=groups)  33 us
    pallas_call x1, Pallas kernels, attend(): pl.pallas_call(attend_kernel, grid=(heads // HEADS_STEP,), in_specs=[pl.B...  13.4 us
    all_to_all x1, waiting for transfers between devices, spread_sum(): lax.all_to_all(copies, axis, 0, 0, axis_index_groups=groups)  5.36 us
    all_to_all x1, starting transfers between devices, spread_sum(): lax.all_to_all(copies, axis, 0, 0, axis_index_groups=groups)  4.58 us
    ppermute x1, starting transfers between devices, body(): back = lax.ppermute(joined, 'seq', backward)  3.79 us
    ppermute x1, starting transfers between devices, body(): far_k = lax.ppermute(k_own, 'seq', forward)  3.49 us
    ppermute x1, starting transfers between devices, body(): far_v = lax.ppermute(v_own, 'seq', forward)  3.49 us
    ppermute x1, waiting for transfers between devices, body(): far_v = lax.ppermute(v_own, 'seq', forward)  3.29 us
  transfers between devices with their start and end apart: 9, of which 4 were waited for; matrix products, arithmetic and copies ran while one was open for 4% of the time, Pallas kernels for 0%

profile of v1, /device:TPU:32, one launch (start us, length us, event | category | flops | bytes accessed | tf_op | source)
XLA Modules:
  0.0 88.2 jit_solution(2526922755130704980)
XLA Ops:
  0.6 3.5 %collective-permute-start = (bf16[256,512]{1,0:T(8,128)(2,1)}, bf16[256,512]{1,0:T(8,128)(2,1)S(1)}, u32[]{:S(2)}, u32[]{:S(2)}) collective-permute-start(bf16[256,512]{1,0:T(8,128)(2,1)} %bitcast.22), channel_id=1, source_target_pairs={{0,2},{1,3},{2,4},{3,5},{4,6},{5,7},{6,8},{7,9},{8,10},{9,11},{10,... | collective-permute-start | bytes 786440 | tf_op jit(solution)/shard_map/ppermute | solution.py:253
  4.1 1.5 %collective-permute-start.2 = (bf16[256,512]{1,0:T(8,128)(2,1)}, bf16[256,512]{1,0:T(8,128)(2,1)S(1)}, u32[]{:S(2)}, u32[]{:S(2)}) collective-permute-start(bf16[256,512]{1,0:T(8,128)(2,1)} %bitcast.23), channel_id=1, source_target_pairs={{0,1},{2,3},{4,5},{6,7},{8,9},{10,11},{12,13},{14,15},{16,17},{18,... | collective-permute-start | bytes 786440 | tf_op jit(solution)/shard_map/ppermute | solution.py:255
  5.6 3.5 %collective-permute-start.1 = (bf16[256,512]{1,0:T(8,128)(2,1)}, bf16[256,512]{1,0:T(8,128)(2,1)S(1)}, u32[]{:S(2)}, u32[]{:S(2)}) collective-permute-start(bf16[256,512]{1,0:T(8,128)(2,1)} %bitcast.25), channel_id=1, source_target_pairs={{0,2},{1,3},{2,4},{3,5},{4,6},{5,7},{6,8},{7,9},{8,10},{9,11},{10,... | collective-permute-start | bytes 786440 | tf_op jit(solution)/shard_map/ppermute | solution.py:254
  9.1 1.3 %collective-permute-start.3 = (bf16[256,512]{1,0:T(8,128)(2,1)}, bf16[256,512]{1,0:T(8,128)(2,1)S(1)}, u32[]{:S(2)}, u32[]{:S(2)}) collective-permute-start(bf16[256,512]{1,0:T(8,128)(2,1)} %bitcast.26), channel_id=1, source_target_pairs={{0,1},{2,3},{4,5},{6,7},{8,9},{10,11},{12,13},{14,15},{16,17},{18,... | collective-permute-start | bytes 786440 | tf_op jit(solution)/shard_map/ppermute | solution.py:256
  10.4 1.0 %reduce-window_clone.1 = s32[1,128]{1,0:T(1,128)S(1)} reduce-window(s32[1,128]{1,0:T(1,128)} %param.11, s32[]{:T(128)} %constant.45.clone.1), window={size=1x128 pad=0_0x127_0}, to_apply=%region_0.1 | reduce-window | flops 16256 | bytes 1028 | tf_op jit(solution)/shard_map/reduce-window.clone
  11.4 0.7 subtract_bitcast_fusion
  12.3 0.7 tile.9.dstart
  13.1 0.8 collective-permute-done.far_k
  13.9 1.3 %collective-permute-start.4 = (bf16[256,512]{1,0:T(8,128)(2,1)S(1)}, bf16[256,512]{1,0:T(8,128)(2,1)S(1)}, u32[]{:S(2)}, u32[]{:S(2)}) collective-permute-start(bf16[256,512]{1,0:T(8,128)(2,1)S(1)} %collective-permute-done.far_k), channel_id=1, source_target_pairs={{1,0},{3,2},{5,4},{7,6},{9,8},{11,10},{13,12},{15,14},{17,16},{19,... | collective-permute-start | bytes 786440 | tf_op jit(solution)/shard_map/ppermute | solution.py:257
  15.2 3.3 %collective-permute-done.1.far_v = bf16[256,512]{1,0:T(8,128)(2,1)S(1)} collective-permute-done((bf16[256,512]{1,0:T(8,128)(2,1)}, bf16[256,512]{1,0:T(8,128)(2,1)S(1)}, u32[]{:S(2)}, u32[]{:S(2)}) %collective-permute-start.1) | collective-permute-done | bytes 262176 | tf_op jit(solution)/shard_map/ppermute | solution.py:254
  18.5 1.3 %collective-permute-start.5 = (bf16[256,512]{1,0:T(8,128)(2,1)S(1)}, bf16[256,512]{1,0:T(8,128)(2,1)S(1)}, u32[]{:S(2)}, u32[]{:S(2)}) collective-permute-start(bf16[256,512]{1,0:T(8,128)(2,1)S(1)} %collective-permute-done.1.far_v), channel_id=1, source_target_pairs={{1,0},{3,2},{5,4},{7,6},{9,8},{11,10},{13,12},{15,14},{17,16},{19,... | collective-permute-start | bytes 786440 | tf_op jit(solution)/shard_map/ppermute | solution.py:258
  19.8 0.6 pad_add_fusion.info
  20.4 1.5 %collective-permute-done.5.near_vb = bf16[256,512]{1,0:T(8,128)(2,1)S(1)} collective-permute-done((bf16[256,512]{1,0:T(8,128)(2,1)S(1)}, bf16[256,512]{1,0:T(8,128)(2,1)S(1)}, u32[]{:S(2)}, u32[]{:S(2)}) %collective-permute-start.5) | collective-permute-done | bytes 262176 | tf_op jit(solution)/shard_map/ppermute | solution.py:258
  22.0 0.7 copy-done.7
  22.7 13.4 %shard_map.110 = (bf16[256,4096]{1,0:T(8,128)(2,1)}, f32[2,256,512]{2,1,0:T(8,128)}, bf16[2,256,512]{2,1,0:T(8,128)(2,1)}, bf16[2,256,512]{2,1,0:T(8,128)(2,1)}, f32[8,4,2,128]{3,2,1,0:T(2,128)}) custom-call(s32[5]{0:T(128)} %pad_add_fusion.info, s32[4,256]{1,0:T(4,128)} %tile.9.dstart, f32[1,512]{1,0:T(1,128)} %bitcast.14, f32[1,512]{1,0:T(1,128)} %bitcast.16, ...), custom_call_target="tpu_custom_call" | custom-call | flops 6039797760 | bytes 8388608 | tf_op jit(solution)/shard_map/pallas_call | solution.py:171
  36.1 13.7 %all_to_all.15 = f32[8,4,2,128]{3,2,1,0:T(2,128)S(1)} all-to-all(f32[8,4,2,128]{3,2,1,0:T(2,128)} %get-tuple-element.21), channel_id=1, replica_groups={{0,1,2,3,4,5,6,7},{8,9,10,11,12,13,14,15},{16,17,18,19,20,21,22,23},{24..., dimensions={0} | all-to-all | bytes 65536 | tf_op jit(solution)/shard_map/all_to_all | solution.py:232
  49.9 0.6 broadcast_in_dim.55
  50.5 4.6 %all-to-all-start.1 = ((f32[4,4,2,128]{3,1,2,0:T(4,128)}), f32[4,4,2,128]{3,1,2,0:T(4,128)S(1)}, u32[]{:S(2)}, u32[]{:S(2)}) async-start(f32[4,4,2,128]{3,1,2,0:T(4,128)} %broadcast_in_dim.55), calls=%async_computation.1 | async-start | bytes 32768 | tf_op jit(solution)/shard_map/all_to_all | solution.py:232
  55.1 5.4 %all-to-all-done.1 = f32[4,4,2,128]{3,1,2,0:T(4,128)S(1)} async-done(((f32[4,4,2,128]{3,1,2,0:T(4,128)}), f32[4,4,2,128]{3,1,2,0:T(4,128)S(1)}, u32[]{:S(2)}, u32[]{:S(2)}) %all-to-all-start.1) | async-done | bytes 16416 | tf_op jit(solution)/shard_map/all_to_all | solution.py:232
  60.5 1.4 %add_convert_fusion = bf16[2,256,512]{2,1,0:T(8,128)(2,1)S(1)} fusion(bf16[2,256,512]{2,1,0:T(8,128)(2,1)S(1)} %collective-permute-done.6.swapped, bf16[2,256,512]{2,1,0:T(8,128)(2,1)} %get-tuple-element.27, pred[]{:T(512)S(6)} %eq.5), kind=kLoop, calls=%fused_computation | loop fusion | flops 1310720 | bytes 1572865 | tf_op jit(solution)/shard_map/convert_element_type | solution.py:283
  61.9 3.8 %collective-permute-start.7 = (bf16[2,256,512]{2,1,0:T(8,128)(2,1)S(1)}, bf16[2,256,512]{2,1,0:T(8,128)(2,1)S(1)}, u32[]{:S(2)}, u32[]{:S(2)}) collective-permute-start(bf16[2,256,512]{2,1,0:T(8,128)(2,1)S(1)} %add_convert_fusion), channel_id=1, source_target_pairs={{2,0},{3,1},{4,2},{5,3},{6,4},{7,5},{8,6},{9,7},{10,8},{11,9},{12,... | collective-permute-start | bytes 1572872 | tf_op jit(solution)/shard_map/ppermute | solution.py:284
  65.7 19.2 %all_to_all.16 = f32[8,4,2,128]{3,2,1,0:T(2,128)S(1)} all-to-all(f32[8,4,2,128]{3,2,1,0:T(2,128)S(1)} %broadcast_in_dim.57), channel_id=1, replica_groups={{0,8,16,24,32,40,48,56},{1,9,17,25,33,41,49,57},{2,10,18,26,34,42,50,58..., dimensions={0} | all-to-all | bytes 65536 | tf_op jit(solution)/shard_map/all_to_all | solution.py:232
  85.0 0.6 slice_multiply_fusion
  85.8 2.3 %shard_map.111 = (bf16[256,512]{1,0:T(8,128)(2,1)}, bf16[256,512]{1,0:T(8,128)(2,1)}) custom-call(s32[1]{0:T(128)} %bitcast.1.even_ref, f32[1,512]{1,0:T(1,128)} %bitcast.15, f32[1,512]{1,0:T(1,128)} %bitcast.17, f32[2,256,512]{2,1,0:T(8,128)} %get-tuple-element.20.own, bf16[2,256,512]{2,1,0:T(8,128)(2,1)} %copy-done, bf16[2,256,512]{2,1,0:T(8,128)(2,1)} %copy-done.1), custom_call_target="tpu_custom_call" | custom-call | tf_op jit(solution)/shard_map/pallas_call | solution.py:221
  (34 shorter events, 0.8 us)
Async XLA Ops:
  0.6 13.3 %collective-permute-start = (bf16[256,512]{1,0:T(8,128)(2,1)}, bf16[256,512]{1,0:T(8,128)(2,1)S(1)}, u32[]{:S(2)}, u32[]{:S(2)}) collective-permute-start(bf16[256,512]{1,0:T(8,128)(2,1)} %bitcast.22), channel_id=1, source_target_pairs={{0,2},{1,3},{2,4},{3,5},{4,6},{5,7},{6,8},{7,9},{8,10},{9,11},{10,... | collective-permute-start | bytes 786440 | tf_op jit(solution)/shard_map/ppermute | solution.py:253
  4.1 16.3 %collective-permute-start.2 = (bf16[256,512]{1,0:T(8,128)(2,1)}, bf16[256,512]{1,0:T(8,128)(2,1)S(1)}, u32[]{:S(2)}, u32[]{:S(2)}) collective-permute-start(bf16[256,512]{1,0:T(8,128)(2,1)} %bitcast.23), channel_id=1, source_target_pairs={{0,1},{2,3},{4,5},{6,7},{8,9},{10,11},{12,13},{14,15},{16,17},{18,... | collective-permute-start | bytes 786440 | tf_op jit(solution)/shard_map/ppermute | solution.py:255
  5.6 12.9 %collective-permute-start.1 = (bf16[256,512]{1,0:T(8,128)(2,1)}, bf16[256,512]{1,0:T(8,128)(2,1)S(1)}, u32[]{:S(2)}, u32[]{:S(2)}) collective-permute-start(bf16[256,512]{1,0:T(8,128)(2,1)} %bitcast.25), channel_id=1, source_target_pairs={{0,2},{1,3},{2,4},{3,5},{4,6},{5,7},{6,8},{7,9},{8,10},{9,11},{10,... | collective-permute-start | bytes 786440 | tf_op jit(solution)/shard_map/ppermute | solution.py:254
  9.1 11.3 %collective-permute-start.3 = (bf16[256,512]{1,0:T(8,128)(2,1)}, bf16[256,512]{1,0:T(8,128)(2,1)S(1)}, u32[]{:S(2)}, u32[]{:S(2)}) collective-permute-start(bf16[256,512]{1,0:T(8,128)(2,1)} %bitcast.26), channel_id=1, source_target_pairs={{0,1},{2,3},{4,5},{6,7},{8,9},{10,11},{12,13},{14,15},{16,17},{18,... | collective-permute-start | bytes 786440 | tf_op jit(solution)/shard_map/ppermute | solution.py:256
  13.9 8.0 %copy-start.2 = (bf16[256,512]{1,0:T(8,128)(2,1)}, bf16[256,512]{1,0:T(8,128)(2,1)S(1)}, u32[]{:S(2)}) copy-start(bf16[256,512]{1,0:T(8,128)(2,1)S(1)} %collective-permute-done.far_k) | copy-start | bytes 786436
  13.9 6.5 %collective-permute-start.4 = (bf16[256,512]{1,0:T(8,128)(2,1)S(1)}, bf16[256,512]{1,0:T(8,128)(2,1)S(1)}, u32[]{:S(2)}, u32[]{:S(2)}) collective-permute-start(bf16[256,512]{1,0:T(8,128)(2,1)S(1)} %collective-permute-done.far_k), channel_id=1, source_target_pairs={{1,0},{3,2},{5,4},{7,6},{9,8},{11,10},{13,12},{15,14},{17,16},{19,... | collective-permute-start | bytes 786440 | tf_op jit(solution)/shard_map/ppermute | solution.py:257
  18.5 3.4 %copy-start.4 = (bf16[256,512]{1,0:T(8,128)(2,1)}, bf16[256,512]{1,0:T(8,128)(2,1)S(1)}, u32[]{:S(2)}) copy-start(bf16[256,512]{1,0:T(8,128)(2,1)S(1)} %collective-permute-done.1.far_v) | copy-start | bytes 786436
  18.5 3.4 %collective-permute-start.5 = (bf16[256,512]{1,0:T(8,128)(2,1)S(1)}, bf16[256,512]{1,0:T(8,128)(2,1)S(1)}, u32[]{:S(2)}, u32[]{:S(2)}) collective-permute-start(bf16[256,512]{1,0:T(8,128)(2,1)S(1)} %collective-permute-done.1.far_v), channel_id=1, source_target_pairs={{1,0},{3,2},{5,4},{7,6},{9,8},{11,10},{13,12},{15,14},{17,16},{19,... | collective-permute-start | bytes 786440 | tf_op jit(solution)/shard_map/ppermute | solution.py:258
  20.4 1.5 %copy-start.3 = (bf16[256,512]{1,0:T(8,128)(2,1)}, bf16[256,512]{1,0:T(8,128)(2,1)S(1)}, u32[]{:S(2)}) copy-start(bf16[256,512]{1,0:T(8,128)(2,1)S(1)} %collective-permute-done.2.near_ka) | copy-start | bytes 786436
  20.4 1.5 %copy-start.5 = (bf16[256,512]{1,0:T(8,128)(2,1)}, bf16[256,512]{1,0:T(8,128)(2,1)S(1)}, u32[]{:S(2)}) copy-start(bf16[256,512]{1,0:T(8,128)(2,1)S(1)} %collective-permute-done.3.near_va) | copy-start | bytes 786436
  20.4 1.5 %copy-start.6 = (bf16[256,512]{1,0:T(8,128)(2,1)}, bf16[256,512]{1,0:T(8,128)(2,1)S(1)}, u32[]{:S(2)}) copy-start(bf16[256,512]{1,0:T(8,128)(2,1)S(1)} %collective-permute-done.4.near_kb) | copy-start | bytes 786436
  21.9 0.7 copy-start.7
  49.8 10.7 %collective-permute-start.6 = (bf16[2,256,512]{2,1,0:T(8,128)(2,1)}, bf16[2,256,512]{2,1,0:T(8,128)(2,1)S(1)}, u32[]{:S(2)}, u32[]{:S(2)}) collective-permute-start(bf16[2,256,512]{2,1,0:T(8,128)(2,1)} %get-tuple-element.24), channel_id=1, source_target_pairs={{0,1},{2,3},{4,5},{6,7},{8,9},{10,11},{12,13},{14,15},{16,17},{18,... | collective-permute-start | bytes 1572872 | tf_op jit(solution)/shard_map/ppermute | solution.py:279
  50.5 9.9 %all-to-all-start.1 = ((f32[4,4,2,128]{3,1,2,0:T(4,128)}), f32[4,4,2,128]{3,1,2,0:T(4,128)S(1)}, u32[]{:S(2)}, u32[]{:S(2)}) async-start(f32[4,4,2,128]{3,1,2,0:T(4,128)} %broadcast_in_dim.55), calls=%async_computation.1 | async-start | bytes 32768 | tf_op jit(solution)/shard_map/all_to_all | solution.py:232
  60.5 25.2 %copy-start = (bf16[2,256,512]{2,1,0:T(8,128)(2,1)}, bf16[2,256,512]{2,1,0:T(8,128)(2,1)S(1)}, u32[]{:S(2)}) copy-start(bf16[2,256,512]{2,1,0:T(8,128)(2,1)S(1)} %collective-permute-done.6.swapped) | copy-start | bytes 1572868
  61.9 23.1 %collective-permute-start.7 = (bf16[2,256,512]{2,1,0:T(8,128)(2,1)S(1)}, bf16[2,256,512]{2,1,0:T(8,128)(2,1)S(1)}, u32[]{:S(2)}, u32[]{:S(2)}) collective-permute-start(bf16[2,256,512]{2,1,0:T(8,128)(2,1)S(1)} %add_convert_fusion), channel_id=1, source_target_pairs={{2,0},{3,1},{4,2},{5,3},{6,4},{7,5},{8,6},{9,7},{10,8},{11,9},{12,... | collective-permute-start | bytes 1572872 | tf_op jit(solution)/shard_map/ppermute | solution.py:284
  85.0 0.8 copy-start.1

commit v2 on v1

v2 whole, which is shorter than its diff:
```python
import functools
import math

import jax
import jax.numpy as jnp
from jax import lax
from jax.experimental import pallas as pl
from jax.experimental.pallas import tpu as pltpu
from jax.sharding import PartitionSpec as P

HD = 128
REACH = 2
DOC_MOST = 512
QT = 64
KG = 64
LANES = 256
NEG = -1e30
F32 = jnp.float32
BF16 = jnp.bfloat16
NT = (((1,), (1,)), ((), ()))


def attend_kernel(
    info, dstart, kscale, vscale, q_ref, g_ref, k_own, v_own,
    far_k, far_v, near_ka, near_va, near_kb, near_vb,
    dq_ref, own_ref, two_ref, one_ref, sums_ref,
    bias, k_raw, v_raw, k_win, v_win, dk_acc, dv_acc,
):
    tok, width = k_own.shape
    heads = width // HD
    front = REACH * tok
    packed = LANES // QT
    parts = q_ref.shape[1] // width // packed
    tiles = tok // QT
    most = (DOC_MOST + QT) // KG
    inv_root = 1.0 / math.sqrt(HD)
    log2_scale = inv_root * math.log2(math.e)
    tile = pl.program_id(0)

    @pl.when(tile == 0)
    def _():
        even = info[tiles] == 0
        for head in range(heads):
            cols = slice(head * HD, (head + 1) * HD)
            k_raw[head, :tok] = far_k[:, cols]
            v_raw[head, :tok] = far_v[:, cols]
            k_raw[head, tok:front] = jnp.where(even, near_kb[:, cols], near_ka[:, cols])
            v_raw[head, tok:front] = jnp.where(even, near_vb[:, cols], near_va[:, cols])
            k_raw[head, front:] = k_own[:, cols]
            v_raw[head, front:] = v_own[:, cols]
            k_win[head] = (k_raw[head].astype(F32) * kscale[:, cols]).astype(BF16)
            v_win[head] = (v_raw[head].astype(F32) * vscale[:, cols]).astype(BF16)
        dk_acc[...] = jnp.zeros_like(dk_acc)
        dv_acc[...] = jnp.zeros_like(dv_acc)

    reach = front + QT
    k_pos = lax.broadcasted_iota(jnp.int32, (reach, LANES), 0)
    lane = lax.broadcasted_iota(jnp.int32, (reach, LANES), 1) % QT
    start = dstart[pl.ds(tile, 1), :] - tile * QT
    bias[...] = jnp.where((k_pos >= start) & (k_pos <= lane + front), 0.0, NEG)

    def one_tile(units):
        count = units * KG
        low = pl.multiple_of(front + (tile + 1) * QT - count, KG)
        rows = pl.ds(low, count)
        mask = bias[front + QT - count :, :]

        keys_ts = [k_win[h, rows, :].T for h in range(heads)]
        groups = heads * parts
        st = [dict() for _ in range(groups)]
        totals = [None] * heads

        def load(x):
            at = range(x * packed, (x + 1) * packed)
            cols = [slice(c * HD, (c + 1) * HD) for c in at]
            st[x]["q"] = jnp.concatenate([q_ref[:, c] for c in cols], axis=0)
            st[x]["g"] = jnp.concatenate([g_ref[:, c] for c in cols], axis=0)

        def mm_s(x):
            load(x)
            st[x]["s"] = lax.dot_general(k_win[x // parts, rows, :], st[x]["q"], NT, preferred_element_type=F32)

        def mm_d(x):
            st[x]["d"] = lax.dot_general(v_win[x // parts, rows, :], st[x]["g"], NT, preferred_element_type=F32)

        def p1(x):
            st[x]["s"] = st[x]["s"] * log2_scale + mask
            st[x]["m"] = jnp.max(st[x]["s"], axis=0, keepdims=True)

        def p2(x):
            e = jnp.exp2(st[x]["s"] - st[x]["m"])
            inv = 1.0 / jnp.sum(e, axis=0, keepdims=True)
            st[x]["delta"] = jnp.sum(e * st[x]["d"], axis=0, keepdims=True) * inv
            st[x]["e"] = e
            st[x]["inv"] = inv

        def p3(x):
            w = st[x]["e"] * st[x]["inv"]
            st[x]["p"] = w.astype(BF16)
            st[x]["t"] = (w * (st[x]["d"] - st[x]["delta"])).astype(BF16)

        def mm_v(x):
            st[x]["dv"] = jnp.dot(st[x]["p"], st[x]["g"], preferred_element_type=F32)

        def mm_k(x):
            st[x]["dk"] = jnp.dot(st[x]["t"], st[x]["q"], preferred_element_type=F32)

        def mm_q(x):
            dq_t = jnp.dot(keys_ts[x // parts], st[x]["t"], preferred_element_type=F32) * inv_root
            dq = dq_t.T.astype(BF16)
            for i in range(packed):
                c = (x * packed + i) * HD
                dq_ref[:, c : c + HD] = dq[i * QT : (i + 1) * QT]

        def acc(x):
            head = x // parts
            dk, dv = st[x]["dk"], st[x]["dv"]
            if totals[head] is not None:
                dk = dk + totals[head][0]
                dv = dv + totals[head][1]
            totals[head] = (dk, dv)
            if x % parts == parts - 1:
                dk_acc[head, rows, :] += dk
                dv_acc[head, rows, :] += dv

        for turn in range(-1, groups + 2):
            for name, x in ((mm_s, turn + 1), (mm_k, turn - 2), (p2, turn), (mm_d, turn + 1), (mm_q, turn - 2), (acc, turn - 2), (p1, turn + 1), (p3, turn - 1), (mm_v, turn - 1)):
                if 0 <= x < groups:
                    name(x)

    for static in range(1, most + 1):
        pl.when(info[tile] == static)(functools.partial(one_tile, static))

    @pl.when(tile == tiles - 1)
    def _():
        for head in range(heads):
            cols = slice(head * HD, (head + 1) * HD)
            dk = dk_acc[head] * inv_root
            dv = dv_acc[head]
            own_ref[0, :, cols] = dk[front:]
            own_ref[1, :, cols] = dv[front:]
            two_ref[0, :, cols] = dk[:tok].astype(BF16)
            two_ref[1, :, cols] = dv[:tok].astype(BF16)
            one_ref[0, :, cols] = dk[tok:front].astype(BF16)
            one_ref[1, :, cols] = dv[tok:front].astype(BF16)
            k_sum = jnp.sum(dk * k_raw[head].astype(F32), axis=0, keepdims=True)
            v_sum = jnp.sum(dv * v_raw[head].astype(F32), axis=0, keepdims=True)
            for copy in range(sums_ref.shape[0]):
                sums_ref[copy, head, 0:1, :] = k_sum
                sums_ref[copy, head, 1:2, :] = v_sum


def attend(info, dstart, kscale, vscale, q, g, k_own, v_own, *received):
    tok, width = k_own.shape
    span = (REACH + 1) * tok
    tiles = tok // QT
    heads = width // HD

    def whole(*shape):
        return pl.BlockSpec(shape, lambda j: (0,) * len(shape))

    strip = pl.BlockSpec((QT, q.shape[1]), lambda j: (j, 0))
    vec = whole(1, width)
    pair = whole(2, tok, width)
    out_shape = (
        jax.ShapeDtypeStruct(q.shape, BF16),
        jax.ShapeDtypeStruct((2, tok, width), F32),
        jax.ShapeDtypeStruct((2, tok, width), BF16),
        jax.ShapeDtypeStruct((2, tok, width), BF16),
        jax.ShapeDtypeStruct((8, heads, 2, HD), F32),
    )
    window = pltpu.VMEM((heads, span, HD), BF16)
    total = pltpu.VMEM((heads, span, HD), F32)
    return pl.pallas_call(
        attend_kernel,
        grid=(tiles,),
        in_specs=[
            pl.BlockSpec(memory_space=pltpu.SMEM),
            whole(tiles, LANES),
            vec,
            vec,
            strip,
            strip,
        ]
        + [whole(tok, width)] * 8,
        out_specs=(strip, pair, pair, pair, whole(8, heads, 2, HD)),
        out_shape=out_shape,
        scratch_shapes=[
            pltpu.VMEM((REACH * tok + QT, LANES), F32),
            window,
            window,
            window,
            window,
            total,
            total,
        ],
        compiler_params=pltpu.CompilerParams(vmem_limit_bytes=58 * 2**20),
        cost_estimate=pl.CostEstimate(
            flops=heads * 8 * 256 * 576 * 128 * 10, bytes_accessed=heads * 2**21, transcendentals=0
        ),
    )(info, dstart, kscale, vscale, q, g, k_own, v_own, *received)


def finish_kernel(even_ref, kscale, vscale, own, swapped, back, gk_ref, gv_ref):
    even = even_ref[0] == 0
    for half, (out, scale) in enumerate(((gk_ref, kscale), (gv_ref, vscale))):
        near = jnp.where(even, swapped[half].astype(F32), 0.0)
        total = own[half] + near + back[half].astype(F32)
        out[...] = (total * scale[...]).astype(BF16)


def finish(parity, kscale, vscale, own, swapped, back):
    _, tok, width = own.shape
    step = 2 * HD
    pair = pl.BlockSpec((2, tok, step), lambda i: (0, 0, i))
    vec = pl.BlockSpec((1, step), lambda i: (0, i))
    out = pl.BlockSpec((tok, step), lambda i: (0, i))
    return pl.pallas_call(
        finish_kernel,
        grid=(width // step,),
        in_specs=[pl.BlockSpec(memory_space=pltpu.SMEM), vec, vec, pair, pair, pair],
        out_specs=(out, out),
        out_shape=(jax.ShapeDtypeStruct((tok, width), BF16),) * 2,
        compiler_params=pltpu.CompilerParams(vmem_limit_bytes=58 * 2**20),
    )(parity[None], kscale, vscale, own, swapped, back)


def spread_sum(copies, axis, groups):
    return jnp.sum(lax.all_to_all(copies, axis, 0, 0, axis_index_groups=groups), axis=0)


def repeated(value, count):
    return jnp.broadcast_to(value[None], (count,) + value.shape)


def body(queries, key_base, value_base, out_grad, doc_lengths, key_scale, value_scale):
    tok = queries.shape[1]
    size = lax.axis_size("seq")
    heads = key_base.shape[2] // HD
    group = queries.shape[2] // heads
    k_own = key_base[0]
    v_own = value_base[0]
    to_odd = [(i, i + 1) for i in range(0, size, 2)]
    to_even = [(i + 1, i) for i in range(0, size, 2)]
    forward = [(i, i + 2) for i in range(size - 2)]
    backward = [(i + 2, i) for i in range(size - 2)]
    device_pos = lax.axis_index("seq")
    parity = device_pos % 2

    far_k = lax.ppermute(k_own, "seq", forward)
    far_v = lax.ppermute(v_own, "seq", forward)
    near_ka = lax.ppermute(k_own, "seq", to_odd)
    near_va = lax.ppermute(v_own, "seq", to_odd)
    near_kb = lax.ppermute(far_k, "seq", to_even)

    lengths = doc_lengths[0]
    starts = jnp.cumsum(lengths) - lengths
    first_key = (device_pos - REACH) * tok
    q_pos = device_pos * tok + jnp.arange(tok, dtype=jnp.int32)
    doc_start = jnp.max(jnp.where(starts[None, :] <= q_pos[:, None], starts[None, :], 0), axis=1)
    rel = (doc_start - first_key).reshape(tok // QT, QT)
    ends = REACH * tok + (jnp.arange(tok // QT, dtype=jnp.int32) + 1) * QT
    units = jnp.clip((ends - rel[:, 0] + KG - 1) // KG, 1, (DOC_MOST + QT) // KG)
    info = jnp.concatenate([units, parity[None]]).astype(jnp.int32)
    dstart = jnp.tile(rel, (1, LANES // QT))

    far_v, near_kb, info, dstart = lax.optimization_barrier((far_v, near_kb, info, dstart))
    near_vb = lax.ppermute(far_v, "seq", to_even)
    dq, own, two_back, one_back, sums = attend(
        info, dstart, key_scale[None], value_scale[None], queries[0], out_grad[0],
        k_own, v_own, far_k, far_v, near_ka, near_va, near_kb, near_vb,
    )
    rows = [[a * 8 + b for b in range(8)] for a in range(size // 8)]
    columns = [[a * 8 + b for a in range(size // 8)] for b in range(8)]
    swapped = lax.ppermute(one_back, "seq", to_odd + to_even)
    partial = spread_sum(sums, "seq", rows)
    partial, swapped, two_back = lax.optimization_barrier((partial, swapped, two_back))
    swapped_odd = jnp.where(parity == 1, swapped.astype(F32), 0.0)
    joined = (two_back.astype(F32) + swapped_odd).astype(BF16)
    back = lax.ppermute(joined, "seq", backward)
    partial, joined = lax.optimization_barrier((partial, joined))
    partial = spread_sum(repeated(partial, 4), "grp", None)
    totals = spread_sum(repeated(partial, 8), "seq", columns)
    totals, back = lax.optimization_barrier((totals, back))
    grad_key_base, grad_value_base = finish(
        parity, key_scale[None], value_scale[None], own, swapped, back
    )
    norm = math.sqrt(lax.axis_size("grp") * size * tok)
    return (
        dq[None],
        grad_key_base[None],
        grad_value_base[None],
        totals[:, 0].reshape(heads * HD) / norm,
        totals[:, 1].reshape(heads * HD) / norm,
    )


def solution(mesh):
    return jax.shard_map(
        body,
        mesh=mesh,
        in_specs=(
            P("grp", "seq", None),
            P("grp", "seq", None),
            P("grp", "seq", None),
            P("grp", "seq", None),
            P("grp", None),
            P(),
            P(),
        ),
        out_specs=(P("grp", "seq", None), P("grp", "seq", None), P("grp", "seq", None), P(), P()),
        check_vma=False,
    )
```

time: 88.2 us -> 84.2 us (0.955)
  blocking collectives: 33 us -> 29.8 us
  Pallas kernels: 15.7 us -> 12.8 us
  starting transfers between devices: 20.8 us -> 23.3 us
    all_to_all x2, blocking collectives: 33 us -> 29.8 us  [spread_sum(): lax.all_to_all(copies, axis, 0, 0, axis_index_groups=groups)]
    ppermute x1, starting transfers between devices: 3.79 us -> 6.8 us  [body(): back = lax.ppermute(joined, 'seq', backward)]
    pallas_call x1, Pallas kernels: 13.4 us -> 10.5 us  [attend(): pl.pallas_call(attend_kernel, grid=(tiles,), in_specs=[pl.BlockSpec(memor...]
    all_to_all x1, starting transfers between devices: 4.58 us -> 3.53 us  [spread_sum(): lax.all_to_all(copies, axis, 0, 0, axis_index_groups=groups)]
where the time goes in v2:
time: 84.2 us; the launch traced here: 84.1 us
  blocking collectives  29.8 us (35%)
  starting transfers between devices  23.3 us (28%)
  Pallas kernels  12.8 us (15%)
  waiting for transfers between devices  11 us (13%)
  other arithmetic  4.5 us (5%)
  local copies, waits for them, and re-layouts  1.8 us (2%)
  between operations  0.85 us (1%)
    all_to_all x2, blocking collectives, spread_sum(): lax.all_to_all(copies, axis, 0, 0, axis_index_groups=groups)  29.8 us
    pallas_call x1, Pallas kernels, attend(): pl.pallas_call(attend_kernel, grid=(tiles,), in_specs=[pl.BlockSpec(memor...  10.5 us
    ppermute x1, starting transfers between devices, body(): back = lax.ppermute(joined, 'seq', backward)  6.8 us
    all_to_all x1, waiting for transfers between devices, spread_sum(): lax.all_to_all(copies, axis, 0, 0, axis_index_groups=groups)  5.45 us
    all_to_all x1, starting transfers between devices, spread_sum(): lax.all_to_all(copies, axis, 0, 0, axis_index_groups=groups)  3.53 us
    ppermute x1, starting transfers between devices, body(): far_k = lax.ppermute(k_own, 'seq', forward)  3.49 us
    ppermute x1, starting transfers between devices, body(): far_v = lax.ppermute(v_own, 'seq', forward)  3.49 us
    ppermute x1, waiting for transfers between devices, body(): far_v = lax.ppermute(v_own, 'seq', forward)  2.68 us
  transfers between devices with their start and end apart: 9, of which 4 were waited for; matrix products, arithmetic and copies ran while one was open for 4% of the time, Pallas kernels for 0%

profile of v2, /device:TPU:32, one launch (start us, length us, event | category | flops | bytes accessed | tf_op | source)
XLA Modules:
  0.0 84.1 jit_solution(2912842907036614718)
XLA Ops:
  0.6 3.5 %collective-permute-start.1 = (bf16[256,512]{1,0:T(8,128)(2,1)}, bf16[256,512]{1,0:T(8,128)(2,1)S(1)}, u32[]{:S(2)}, u32[]{:S(2)}) collective-permute-start(bf16[256,512]{1,0:T(8,128)(2,1)} %bitcast.22), channel_id=1, source_target_pairs={{0,2},{1,3},{2,4},{3,5},{4,6},{5,7},{6,8},{7,9},{8,10},{9,11},{10,... | collective-permute-start | bytes 786440 | tf_op jit(solution)/shard_map/ppermute | solution.py:250
  4.1 1.5 %collective-permute-start.3 = (bf16[256,512]{1,0:T(8,128)(2,1)}, bf16[256,512]{1,0:T(8,128)(2,1)S(1)}, u32[]{:S(2)}, u32[]{:S(2)}) collective-permute-start(bf16[256,512]{1,0:T(8,128)(2,1)} %bitcast.23), channel_id=1, source_target_pairs={{0,1},{2,3},{4,5},{6,7},{8,9},{10,11},{12,13},{14,15},{16,17},{18,... | collective-permute-start | bytes 786440 | tf_op jit(solution)/shard_map/ppermute | solution.py:252
  5.6 3.5 %collective-permute-start = (bf16[256,512]{1,0:T(8,128)(2,1)}, bf16[256,512]{1,0:T(8,128)(2,1)S(1)}, u32[]{:S(2)}, u32[]{:S(2)}) collective-permute-start(bf16[256,512]{1,0:T(8,128)(2,1)} %bitcast.25), channel_id=1, source_target_pairs={{0,2},{1,3},{2,4},{3,5},{4,6},{5,7},{6,8},{7,9},{8,10},{9,11},{10,... | collective-permute-start | bytes 786440 | tf_op jit(solution)/shard_map/ppermute | solution.py:251
  9.1 1.3 %collective-permute-start.4 = (bf16[256,512]{1,0:T(8,128)(2,1)}, bf16[256,512]{1,0:T(8,128)(2,1)S(1)}, u32[]{:S(2)}, u32[]{:S(2)}) collective-permute-start(bf16[256,512]{1,0:T(8,128)(2,1)} %bitcast.26), channel_id=1, source_target_pairs={{0,1},{2,3},{4,5},{6,7},{8,9},{10,11},{12,13},{14,15},{16,17},{18,... | collective-permute-start | bytes 786440 | tf_op jit(solution)/shard_map/ppermute | solution.py:253
  10.4 1.0 %reduce-window_clone.1 = s32[1,128]{1,0:T(1,128)S(1)} reduce-window(s32[1,128]{1,0:T(1,128)} %param.11, s32[]{:T(128)} %constant.45.clone.1), window={size=1x128 pad=0_0x127_0}, to_apply=%region_0.1 | reduce-window | flops 16256 | bytes 1028 | tf_op jit(solution)/shard_map/reduce-window.clone
  11.4 0.7 subtract_bitcast_fusion
  12.3 0.7 tile.9.dstart
  13.1 0.8 collective-permute-done.1.far_k
  13.9 1.3 %collective-permute-start.2 = (bf16[256,512]{1,0:T(8,128)(2,1)S(1)}, bf16[256,512]{1,0:T(8,128)(2,1)S(1)}, u32[]{:S(2)}, u32[]{:S(2)}) collective-permute-start(bf16[256,512]{1,0:T(8,128)(2,1)S(1)} %collective-permute-done.1.far_k), channel_id=1, source_target_pairs={{1,0},{3,2},{5,4},{7,6},{9,8},{11,10},{13,12},{15,14},{17,16},{19,... | collective-permute-start | bytes 786440 | tf_op jit(solution)/shard_map/ppermute | solution.py:254
  15.2 0.6 pad_add_fusion.info
  15.8 2.7 %collective-permute-done.far_v = bf16[256,512]{1,0:T(8,128)(2,1)S(1)} collective-permute-done((bf16[256,512]{1,0:T(8,128)(2,1)}, bf16[256,512]{1,0:T(8,128)(2,1)S(1)}, u32[]{:S(2)}, u32[]{:S(2)}) %collective-permute-start) | collective-permute-done | bytes 262176 | tf_op jit(solution)/shard_map/ppermute | solution.py:251
  18.5 1.3 %collective-permute-start.5 = (bf16[256,512]{1,0:T(8,128)(2,1)S(1)}, bf16[256,512]{1,0:T(8,128)(2,1)S(1)}, u32[]{:S(2)}, u32[]{:S(2)}) collective-permute-start(bf16[256,512]{1,0:T(8,128)(2,1)S(1)} %collective-permute-done.far_v), channel_id=1, source_target_pairs={{1,0},{3,2},{5,4},{7,6},{9,8},{11,10},{13,12},{15,14},{17,16},{19,... | collective-permute-start | bytes 786440 | tf_op jit(solution)/shard_map/ppermute | solution.py:268
  19.9 2.1 %collective-permute-done.5.near_vb = bf16[256,512]{1,0:T(8,128)(2,1)S(1)} collective-permute-done((bf16[256,512]{1,0:T(8,128)(2,1)S(1)}, bf16[256,512]{1,0:T(8,128)(2,1)S(1)}, u32[]{:S(2)}, u32[]{:S(2)}) %collective-permute-start.5) | collective-permute-done | bytes 262176 | tf_op jit(solution)/shard_map/ppermute | solution.py:268
  22.0 0.7 copy-done.7
  22.7 10.5 %shard_map.110 = (bf16[256,4096]{1,0:T(8,128)(2,1)}, f32[2,256,512]{2,1,0:T(8,128)}, bf16[2,256,512]{2,1,0:T(8,128)(2,1)}, bf16[2,256,512]{2,1,0:T(8,128)(2,1)}, f32[8,4,2,128]{3,2,1,0:T(2,128)}) custom-call(s32[5]{0:T(128)} %pad_add_fusion.info, s32[4,256]{1,0:T(4,128)} %tile.9.dstart, f32[1,512]{1,0:T(1,128)} %bitcast.14, f32[1,512]{1,0:T(1,128)} %bitcast.16, ...), custom_call_target="tpu_custom_call" | custom-call | flops 6039797760 | bytes 8388608 | tf_op jit(solution)/shard_map/pallas_call | solution.py:174
  33.1 0.7 collective-permute-start.6
  33.8 3.5 %all-to-all-start = ((f32[8,4,2,128]{3,2,1,0:T(2,128)}), f32[8,4,2,128]{3,2,1,0:T(2,128)S(1)}, u32[]{:S(2)}, u32[]{:S(2)}) async-start(f32[8,4,2,128]{3,2,1,0:T(2,128)} %get-tuple-element.28), calls=%async_computation | async-start | bytes 65536 | tf_op jit(solution)/shard_map/all_to_all | solution.py:229
  37.3 5.4 %all-to-all-done = f32[8,4,2,128]{3,2,1,0:T(2,128)S(1)} async-done(((f32[8,4,2,128]{3,2,1,0:T(2,128)}), f32[8,4,2,128]{3,2,1,0:T(2,128)S(1)}, u32[]{:S(2)}, u32[]{:S(2)}) %all-to-all-start) | async-done | bytes 32800 | tf_op jit(solution)/shard_map/all_to_all | solution.py:229
  42.8 1.4 %add_convert_fusion = bf16[2,256,512]{2,1,0:T(8,128)(2,1)S(1)} fusion(bf16[2,256,512]{2,1,0:T(8,128)(2,1)S(1)} %collective-permute-done.6.swapped, bf16[2,256,512]{2,1,0:T(8,128)(2,1)} %get-tuple-element.33, pred[]{:T(512)S(6)} %eq.5), kind=kLoop, calls=%fused_computation | loop fusion | flops 1310720 | bytes 1572865 | tf_op jit(solution)/shard_map/convert_element_type | solution.py:279
  44.2 6.8 %collective-permute-start.7 = (bf16[2,256,512]{2,1,0:T(8,128)(2,1)S(1)}, bf16[2,256,512]{2,1,0:T(8,128)(2,1)S(1)}, u32[]{:S(2)}, u32[]{:S(2)}) collective-permute-start(bf16[2,256,512]{2,1,0:T(8,128)(2,1)S(1)} %add_convert_fusion), channel_id=1, source_target_pairs={{2,0},{3,1},{4,2},{5,3},{6,4},{7,5},{8,6},{9,7},{10,8},{11,9},{12,... | collective-permute-start | bytes 1572872 | tf_op jit(solution)/shard_map/ppermute | solution.py:280
  51.0 10.7 %all_to_all.15 = f32[4,4,2,128]{3,1,2,0:T(4,128)S(1)} all-to-all(f32[4,4,2,128]{3,1,2,0:T(4,128)S(1)} %broadcast_in_dim.56), channel_id=1, replica_groups=mesh['grp'=4,'seq'=64] {'grp'}, dimensions={0} | all-to-all | bytes 32768 | tf_op jit(solution)/shard_map/all_to_all | solution.py:229
  61.8 19.1 %all_to_all.16 = f32[8,4,2,128]{3,2,1,0:T(2,128)S(1)} all-to-all(f32[8,4,2,128]{3,2,1,0:T(2,128)S(1)} %broadcast_in_dim.57), channel_id=1, replica_groups={{0,8,16,24,32,40,48,56},{1,9,17,25,33,41,49,57},{2,10,18,26,34,42,50,58..., dimensions={0} | all-to-all | bytes 65536 | tf_op jit(solution)/shard_map/all_to_all | solution.py:229
  80.9 0.6 slice_multiply_fusion
  81.7 2.3 %shard_map.111 = (bf16[256,512]{1,0:T(8,128)(2,1)}, bf16[256,512]{1,0:T(8,128)(2,1)}) custom-call(s32[1]{0:T(128)} %bitcast.3.even_ref, f32[1,512]{1,0:T(1,128)} %bitcast.15, f32[1,512]{1,0:T(1,128)} %bitcast.17, f32[2,256,512]{2,1,0:T(8,128)} %get-tuple-element.27.own, bf16[2,256,512]{2,1,0:T(8,128)(2,1)} %copy-done, bf16[2,256,512]{2,1,0:T(8,128)(2,1)} %copy-done.1), custom_call_target="tpu_custom_call" | custom-call | tf_op jit(solution)/shard_map/pallas_call | solution.py:218
  (34 shorter events, 0.7 us)
Async XLA Ops:
  0.6 13.3 %collective-permute-start.1 = (bf16[256,512]{1,0:T(8,128)(2,1)}, bf16[256,512]{1,0:T(8,128)(2,1)S(1)}, u32[]{:S(2)}, u32[]{:S(2)}) collective-permute-start(bf16[256,512]{1,0:T(8,128)(2,1)} %bitcast.22), channel_id=1, source_target_pairs={{0,2},{1,3},{2,4},{3,5},{4,6},{5,7},{6,8},{7,9},{8,10},{9,11},{10,... | collective-permute-start | bytes 786440 | tf_op jit(solution)/shard_map/ppermute | solution.py:250
  4.1 15.7 %collective-permute-start.3 = (bf16[256,512]{1,0:T(8,128)(2,1)}, bf16[256,512]{1,0:T(8,128)(2,1)S(1)}, u32[]{:S(2)}, u32[]{:S(2)}) collective-permute-start(bf16[256,512]{1,0:T(8,128)(2,1)} %bitcast.23), channel_id=1, source_target_pairs={{0,1},{2,3},{4,5},{6,7},{8,9},{10,11},{12,13},{14,15},{16,17},{18,... | collective-permute-start | bytes 786440 | tf_op jit(solution)/shard_map/ppermute | solution.py:252
  5.6 12.9 %collective-permute-start = (bf16[256,512]{1,0:T(8,128)(2,1)}, bf16[256,512]{1,0:T(8,128)(2,1)S(1)}, u32[]{:S(2)}, u32[]{:S(2)}) collective-permute-start(bf16[256,512]{1,0:T(8,128)(2,1)} %bitcast.25), channel_id=1, source_target_pairs={{0,2},{1,3},{2,4},{3,5},{4,6},{5,7},{6,8},{7,9},{8,10},{9,11},{10,... | collective-permute-start | bytes 786440 | tf_op jit(solution)/shard_map/ppermute | solution.py:251
  9.1 10.7 %collective-permute-start.4 = (bf16[256,512]{1,0:T(8,128)(2,1)}, bf16[256,512]{1,0:T(8,128)(2,1)S(1)}, u32[]{:S(2)}, u32[]{:S(2)}) collective-permute-start(bf16[256,512]{1,0:T(8,128)(2,1)} %bitcast.26), channel_id=1, source_target_pairs={{0,1},{2,3},{4,5},{6,7},{8,9},{10,11},{12,13},{14,15},{16,17},{18,... | collective-permute-start | bytes 786440 | tf_op jit(solution)/shard_map/ppermute | solution.py:253
  13.9 8.0 %copy-start.2 = (bf16[256,512]{1,0:T(8,128)(2,1)}, bf16[256,512]{1,0:T(8,128)(2,1)S(1)}, u32[]{:S(2)}) copy-start(bf16[256,512]{1,0:T(8,128)(2,1)S(1)} %collective-permute-done.1.far_k) | copy-start | bytes 786436
  13.9 4.6 %collective-permute-start.2 = (bf16[256,512]{1,0:T(8,128)(2,1)S(1)}, bf16[256,512]{1,0:T(8,128)(2,1)S(1)}, u32[]{:S(2)}, u32[]{:S(2)}) collective-permute-start(bf16[256,512]{1,0:T(8,128)(2,1)S(1)} %collective-permute-done.1.far_k), channel_id=1, source_target_pairs={{1,0},{3,2},{5,4},{7,6},{9,8},{11,10},{13,12},{15,14},{17,16},{19,... | collective-permute-start | bytes 786440 | tf_op jit(solution)/shard_map/ppermute | solution.py:254
  18.5 3.4 %copy-start.4 = (bf16[256,512]{1,0:T(8,128)(2,1)}, bf16[256,512]{1,0:T(8,128)(2,1)S(1)}, u32[]{:S(2)}) copy-start(bf16[256,512]{1,0:T(8,128)(2,1)S(1)} %collective-permute-done.far_v) | copy-start | bytes 786436
  18.5 3.4 %copy-start.6 = (bf16[256,512]{1,0:T(8,128)(2,1)}, bf16[256,512]{1,0:T(8,128)(2,1)S(1)}, u32[]{:S(2)}) copy-start(bf16[256,512]{1,0:T(8,128)(2,1)S(1)} %collective-permute-done.2.near_kb) | copy-start | bytes 786436
  18.5 3.4 %collective-permute-start.5 = (bf16[256,512]{1,0:T(8,128)(2,1)S(1)}, bf16[256,512]{1,0:T(8,128)(2,1)S(1)}, u32[]{:S(2)}, u32[]{:S(2)}) collective-permute-start(bf16[256,512]{1,0:T(8,128)(2,1)S(1)} %collective-permute-done.far_v), channel_id=1, source_target_pairs={{1,0},{3,2},{5,4},{7,6},{9,8},{11,10},{13,12},{15,14},{17,16},{19,... | collective-permute-start | bytes 786440 | tf_op jit(solution)/shard_map/ppermute | solution.py:268
  19.8 2.1 %copy-start.3 = (bf16[256,512]{1,0:T(8,128)(2,1)}, bf16[256,512]{1,0:T(8,128)(2,1)S(1)}, u32[]{:S(2)}) copy-start(bf16[256,512]{1,0:T(8,128)(2,1)S(1)} %collective-permute-done.3.near_ka) | copy-start | bytes 786436
  19.8 2.1 %copy-start.5 = (bf16[256,512]{1,0:T(8,128)(2,1)}, bf16[256,512]{1,0:T(8,128)(2,1)S(1)}, u32[]{:S(2)}) copy-start(bf16[256,512]{1,0:T(8,128)(2,1)S(1)} %collective-permute-done.4.near_va) | copy-start | bytes 786436
  21.9 0.7 copy-start.7
  33.1 9.7 %collective-permute-start.6 = (bf16[2,256,512]{2,1,0:T(8,128)(2,1)}, bf16[2,256,512]{2,1,0:T(8,128)(2,1)S(1)}, u32[]{:S(2)}, u32[]{:S(2)}) collective-permute-start(bf16[2,256,512]{2,1,0:T(8,128)(2,1)} %get-tuple-element.29), channel_id=1, source_target_pairs={{0,1},{2,3},{4,5},{6,7},{8,9},{10,11},{12,13},{14,15},{16,17},{18,... | collective-permute-start | bytes 1572872 | tf_op jit(solution)/shard_map/ppermute | solution.py:275
  33.8 9.0 %all-to-all-start = ((f32[8,4,2,128]{3,2,1,0:T(2,128)}), f32[8,4,2,128]{3,2,1,0:T(2,128)S(1)}, u32[]{:S(2)}, u32[]{:S(2)}) async-start(f32[8,4,2,128]{3,2,1,0:T(2,128)} %get-tuple-element.28), calls=%async_computation | async-start | bytes 65536 | tf_op jit(solution)/shard_map/all_to_all | solution.py:229
  42.8 38.7 %copy-start = (bf16[2,256,512]{2,1,0:T(8,128)(2,1)}, bf16[2,256,512]{2,1,0:T(8,128)(2,1)S(1)}, u32[]{:S(2)}) copy-start(bf16[2,256,512]{2,1,0:T(8,128)(2,1)S(1)} %collective-permute-done.6.swapped) | copy-start | bytes 1572868
  44.2 36.7 %collective-permute-start.7 = (bf16[2,256,512]{2,1,0:T(8,128)(2,1)S(1)}, bf16[2,256,512]{2,1,0:T(8,128)(2,1)S(1)}, u32[]{:S(2)}, u32[]{:S(2)}) collective-permute-start(bf16[2,256,512]{2,1,0:T(8,128)(2,1)S(1)} %add_convert_fusion), channel_id=1, source_target_pairs={{2,0},{3,1},{4,2},{5,3},{6,4},{7,5},{8,6},{9,7},{10,8},{11,9},{12,... | collective-permute-start | bytes 1572872 | tf_op jit(solution)/shard_map/ppermute | solution.py:280
  80.9 0.8 copy-start.1
